TPU v7x, 32 devices: a whole 2x2x4 slice. The times are simulated.
32 devices in a mesh: rve: 4 (over z), gy: 2 (over x), gz: 4 (over y, core).
Axes of the slice: x: 2, y: 2, z: 4, core: 2. Of those that a mesh axis runs over, the one named last changes fastest.
Arguments:
- strain: float32 [32, 6], P('rve'), may hold values from -6 to 6
- tangent: float32 [32], P('rve'), may hold values from 0.5 to 2
- yield_list: int32 [16], P('rve'), may hold values from 0 to 7, as said below
- destination: int32 [16, 1], P('rve'), may hold values from 0 to 3; in each aligned block of 4 rows (0 to 3, 4 to 7, ...) at most 2 rows name the same one
- phase_map: int32 [4, 8, 32, 128], P('rve', 'gy', 'gz'), may hold values from 0 to 1
- polarization: float32 [4, 3, 6, 8, 32, 128], P('rve', None, None, 'gy', 'gz'), may hold values from -6 to 6
- stencil: float32 [3, 3, 27], replicated, may hold values from -0.6 to 3, as said below
Outputs:
- fields: float32 [4, 8, 3, 8, 32, 128], P('rve', None, None, 'gy', 'gz')
- stress_rows: float32 [16, 6], P('rve')
Inputs may be any that keep to these rules, and one draw needn't show every extreme that they name: `yield_list`: the 4 entries of each macro device are distinct local point numbers, and each device lists 0 and 7. `destination`: among the 4 entries of one macro device, no group is named more than 2 times. stencil[c, d, o] equals stencil[d, c, 26 - o] for all channels and offsets.
All inputs are finite; a program needn't handle non-finite values.
Results may differ from a plain program's by a relative error of at most 0.0003.
Values sent between devices are 32-bit elements; how exact they have to be, the bound alone decides.
A program may use at most 192 MiB of HBM per device.

v0:
```python
import functools

import jax
import jax.numpy as jnp
from jax import lax
from jax.experimental import pallas as pl
from jax.experimental.pallas import tpu as pltpu
from jax.sharding import PartitionSpec as P

CAP = 2
SWEEPS = 6
MESH = pl.DeviceIdType.MESH
TANGENT, TARGET, RANK, LISTED = 6, 7, 8, 9


FULL_PRECISION = lax.Precision.HIGHEST
LOWER_BOUND = 0.05
UPPER_BOUND = 1.95


def padded(block, sides, width):
    for axis, dim in sides:
        count = lax.axis_size(axis)
        forward = [(i, i + 1) for i in range(count - 1)]
        forward.append((count - 1, 0))
        backward = [(target, source) for source, target in forward]
        low = lax.ppermute(
            lax.slice_in_dim(block, block.shape[dim] - width, None, axis=dim), axis, forward
        )
        high = lax.ppermute(lax.slice_in_dim(block, 0, width, axis=dim), axis, backward)
        block = jnp.concatenate([low, block, high], axis=dim)
    return block


def chebyshev_weights(sweep_count):
    centre_value = 0.5 * (UPPER_BOUND + LOWER_BOUND)
    half_width = 0.5 * (UPPER_BOUND - LOWER_BOUND)
    ratio_value = centre_value / half_width
    rho_before = 1.0 / ratio_value
    weights = []
    for sweep_index in range(1, sweep_count):
        rho_after = 1.0 / (2.0 * ratio_value - rho_before)
        weights.append((rho_after * rho_before, 2.0 * rho_after / half_width))
        rho_before = rho_after
    return (1.0 / centre_value, weights)


def trim_margin(values_in, margin_have, margin_want, first_dim):
    excess = margin_have - margin_want
    values_in = lax.slice_in_dim(
        values_in, excess, values_in.shape[first_dim] - excess, axis=first_dim
    )
    return lax.slice_in_dim(
        values_in, excess, values_in.shape[first_dim + 1] - excess, axis=first_dim + 1
    )


def apply_stiffness(field_now, moduli, stencil):
    inner_y = field_now.shape[2] - 2
    inner_z = field_now.shape[3] - 2
    centre_mod = moduli[:, 1 : 1 + inner_y, 1 : 1 + inner_z, :]
    running = [None, None, None]
    for shift_y in (-1, 0, 1):
        for shift_z in (-1, 0, 1):
            shifted = field_now[
                :, :, 1 + shift_y : 1 + shift_y + inner_y, 1 + shift_z : 1 + shift_z + inner_z, :
            ]
            shifted_mod = moduli[
                :, 1 + shift_y : 1 + shift_y + inner_y, 1 + shift_z : 1 + shift_z + inner_z, :
            ]
            for shift_x in (-1, 0, 1):
                if shift_x != 0:
                    rolled = jnp.roll(shifted, -shift_x, axis=4)
                    rolled_mod = jnp.roll(shifted_mod, -shift_x, axis=3)
                else:
                    rolled = shifted
                    rolled_mod = shifted_mod
                offset_index = (shift_y + 1) * 9 + (shift_z + 1) * 3 + (shift_x + 1)
                edge_mod = 0.5 * (centre_mod + rolled_mod)
                weighted = [edge_mod * rolled[:, channel_in] for channel_in in range(3)]
                for channel_out in range(3):
                    mixed = stencil[channel_out, 0, offset_index] * weighted[0]
                    mixed = mixed + stencil[channel_out, 1, offset_index] * weighted[1]
                    mixed = mixed + stencil[channel_out, 2, offset_index] * weighted[2]
                    if running[channel_out] is None:
                        running[channel_out] = mixed
                    else:
                        running[channel_out] = running[channel_out] + mixed
    return jnp.stack(running, axis=1)


def body(strain, tangent, yield_list, destination, phase_map, polarization, stencil):
    groups = lax.axis_size("rve")
    rows_here = strain.shape[0]
    yield_count = yield_list.shape[0]
    picker = (jnp.arange(rows_here, dtype=jnp.int32)[None, :] == yield_list[:, None]).astype(
        jnp.float32
    )
    row_strain = jnp.dot(picker, strain, precision=FULL_PRECISION)
    row_tangent = jnp.dot(picker, tangent, precision=FULL_PRECISION)
    target = destination[:, 0]
    positions = jnp.arange(yield_count, dtype=jnp.int32)
    earlier = (target[:, None] == target[None, :]) & (positions[None, :] < positions[:, None])
    rank_in = jnp.sum(earlier.astype(jnp.int32), axis=1)
    group_ids = jnp.arange(groups, dtype=jnp.int32)
    slot_ids = jnp.arange(CAP, dtype=jnp.int32)
    onehot = (
        (target[None, None, :] == group_ids[:, None, None])
        & (rank_in[None, None, :] == slot_ids[None, :, None])
    ).astype(jnp.float32)
    packet = jnp.einsum("gci,ij->gcj", onehot, row_strain, precision=FULL_PRECISION)
    packet_tangent = (
        jnp.einsum("gci,i->gc", onehot, row_tangent, precision=FULL_PRECISION)
        + 1.0
        - jnp.sum(onehot, axis=2)
    )
    parcel = jnp.concatenate([packet, packet_tangent[:, :, None]], axis=2)
    arrived = lax.all_to_all(parcel, "rve", split_axis=0, concat_axis=0, tiled=True)
    slot_strain = arrived[:, :, :6].reshape(groups * CAP, 6)
    slot_tangent = arrived[:, :, 6].reshape(groups * CAP)
    phase_wide = padded(phase_map[0], (("gy", 0), ("gz", 1)), 2)
    moduli_wide = jnp.where(
        phase_wide[None] == 1, slot_tangent[:, None, None, None], jnp.float32(1.0)
    )
    moduli_core = trim_margin(moduli_wide, 2, 0, 1)
    moduli_one = trim_margin(moduli_wide, 2, 1, 1)
    polar_local = polarization[0]
    centre_diag = jnp.diagonal(stencil[:, :, 13])
    body_force = moduli_core[:, None] * jnp.einsum(
        "cjyzx,lj->lcyzx", polar_local, slot_strain, precision=FULL_PRECISION
    )
    inverse_diag = 1.0 / (centre_diag[None, :, None, None, None] * moduli_core[:, None])
    first_weight, weights = chebyshev_weights(SWEEPS)
    update = first_weight * (body_force * inverse_diag)
    field_now = update
    for old_weight, new_weight in weights:
        wrapped = padded(field_now, (("gy", 2), ("gz", 3)), 1)
        residual_now = body_force - apply_stiffness(wrapped, moduli_one, stencil)
        update = old_weight * update + new_weight * (residual_now * inverse_diag)
        field_now = field_now + update
    coupled = jnp.einsum(
        "cjyzx,lcyzx->lj", polar_local, moduli_core[:, None] * field_now, precision=FULL_PRECISION
    )
    partial_value = coupled + slot_strain * jnp.sum(moduli_core, axis=(1, 2, 3))[:, None]
    total_cells = (
        lax.axis_size("gy")
        * lax.axis_size("gz")
        * field_now.shape[2]
        * field_now.shape[3]
        * field_now.shape[4]
    )
    summed = lax.psum(partial_value, ("gy", "gz")) / total_cells
    returned = lax.all_to_all(
        summed.reshape(groups, CAP, 6), "rve", split_axis=0, concat_axis=0, tiled=True
    )
    stress_rows = jnp.einsum("gci,gcj->ij", onehot, returned, precision=FULL_PRECISION)
    return (field_now[None], stress_rows)


def kernel(
    groups, ngy, ngz,
    strain, tangent, yield_list, destination, stencil, phase, polar,
    fields, rows_out,
    tables, slots, phase_all, force_out, force, matrix, spread, field_now, update,
    mod_mid, mod_low, mod_high, mod_inv, sums, partials, totals,
    table_send, table_recv, phase_send, phase_recv, force_send, force_recv,
    field_send, field_recv, part_send, part_recv, total_send, total_recv,
):
    f32, bf16 = jnp.float32, jnp.bfloat16
    channels, strains = polar.shape[1], polar.shape[2]
    y_here, z_here, nx = polar.shape[3:]
    ny, nz = y_here * ngy, z_here * ngz
    wide = channels * nz
    slot_rows = 3 * wide
    depth = 3 * slot_rows
    listed = yield_list.shape[0]
    loads = groups * CAP
    my_r, my_y, my_z = lax.axis_index("rve"), lax.axis_index("gy"), lax.axis_index("gz")
    my_load = my_y * ngz + my_z

    def turned(base, step, count):
        return lax.rem(base + step + count, count)

    mates = [(dy, dz) for dy in list(range(1, ngy)) + [0] for dz in list(range(1, ngz)) + [0]]
    others = [mate for mate in mates if mate != (0, 0)]

    def mate_id(dy, dz):
        return {"gy": turned(my_y, dy, ngy), "gz": turned(my_z, dz, ngz)}

    def block(dy, dz):
        y_at = turned(my_y, dy, ngy) * y_here
        z_at = pl.multiple_of(turned(my_z, dz, ngz) * z_here, 8)
        return pl.ds(y_at, y_here), pl.ds(z_at, z_here)

    barrier = pltpu.get_barrier_semaphore()
    for dy, dz in others:
        pl.semaphore_signal(barrier, inc=1, device_id=mate_id(dy, dz), device_id_type=MESH)
    for step in range(1, groups):
        pl.semaphore_signal(
            barrier, inc=1, device_id={"rve": turned(my_r, step, groups)}, device_id_type=MESH
        )

    row_ids = lax.broadcasted_iota(jnp.int32, (8, 128), 0)
    lane_ids = lax.broadcasted_iota(jnp.int32, (8, 128), 1)
    table = jnp.zeros((8, 128), f32)
    for i in range(listed):
        point, target = yield_list[i], destination[i, 0]
        rank = jnp.int32(0)
        for k in range(i):
            rank = rank + jnp.where(destination[k, 0] == target, 1, 0)
        values = [strain[point, j] for j in range(strains)]
        values += [tangent[point], target.astype(f32), rank.astype(f32), jnp.float32(1.0)]
        for j, value in enumerate(values):
            table = jnp.where((row_ids == i) & (lane_ids == j), value, table)
    tables[my_r] = table

    pl.semaphore_wait(barrier, len(others) + groups - 1)

    def table_copy(step, owner):
        return pltpu.make_async_remote_copy(
            src_ref=tables.at[my_r], dst_ref=tables.at[owner],
            send_sem=table_send.at[step], recv_sem=table_recv.at[step],
            device_id={"rve": turned(my_r, step, groups)}, device_id_type=MESH,
        )

    def phase_copy(index, dy, dz):
        y_at, z_at = block(dy, dz)
        to_y, to_z = others[index]
        return pltpu.make_async_remote_copy(
            src_ref=phase.at[0], dst_ref=phase_all.at[y_at, z_at],
            send_sem=phase_send.at[index], recv_sem=phase_recv.at[index],
            device_id=mate_id(to_y, to_z), device_id_type=MESH,
        )

    for step in range(1, groups):
        table_copy(step, my_r).start()
    for index in range(len(others)):
        phase_copy(index, 0, 0).start()
    own_y, own_z = block(0, 0)
    phase_all[own_y, own_z, :] = phase[0]

    for step in range(1, groups):
        table_copy(step, turned(my_r, -step, groups)).wait_recv()
    for source in range(groups):
        heard = tables[source]
        named = (heard[:, TARGET : TARGET + 1] == my_r.astype(f32)) & (
            heard[:, LISTED : LISTED + 1] == 1.0
        )
        for rank in range(CAP):
            chosen = named & (heard[:, RANK : RANK + 1] == float(rank))
            line = jnp.sum(jnp.where(chosen, heard, 0.0), axis=0, keepdims=True)
            missing = 1.0 - line[:, LISTED : LISTED + 1]
            line = line + jnp.where(lane_ids[:1] == TANGENT, missing, 0.0)
            at = source * CAP + rank
            slots[at : at + 1, :] = line

    def slot_value(load, index):
        return jnp.broadcast_to(slots[pl.ds(load, 1), :][:, index : index + 1], (8, 128))

    def force_copy(index, dy, dz):
        y_at, z_at = block(dy, dz)
        return pltpu.make_async_remote_copy(
            src_ref=force_out.at[index], dst_ref=force.at[:, y_at, z_at],
            send_sem=force_send.at[index], recv_sem=force_recv.at[index],
            device_id=mate_id(*others[index]), device_id_type=MESH,
        )

    for index, (dy, dz) in enumerate(mates):
        load = turned(my_y, dy, ngy) * ngz + turned(my_z, dz, ngz)
        strain_of = [slot_value(load, j) for j in range(strains)]
        for c in range(channels):
            for y in range(y_here):
                value = polar[0, c, 0, y] * strain_of[0]
                for j in range(1, strains):
                    value = value + polar[0, c, j, y] * strain_of[j]
                if (dy, dz) == (0, 0):
                    force[c, my_y * y_here + y, own_z, :] = value
                else:
                    force_out[index, c, y] = value
        if (dy, dz) != (0, 0):
            force_copy(index, 0, 0).start()

    column = lax.broadcasted_iota(jnp.int32, (1, depth), 1)
    column_y = column // slot_rows
    column_kind = lax.rem(column, slot_rows) // wide
    column_d = lax.rem(column, wide) // nz
    picks = [[(column_y == dy) & (column_d == d) for d in range(channels)] for dy in range(3)]
    z_row = lax.broadcasted_iota(jnp.int32, (nz, depth), 0)
    z_column = lax.rem(lax.broadcasted_iota(jnp.int32, (nz, depth), 1), nz)
    bands = [z_column == lax.rem(z_row + dz - 1 + nz, nz) for dz in range(3)]
    is_low = jnp.broadcast_to(column_kind, (nz, depth)) == 1
    for dx in range(3):
        for c in range(channels):
            values = jnp.zeros((nz, depth), f32)
            for dz in range(3):
                line = jnp.zeros((1, depth), f32)
                for dy in range(3):
                    for d in range(channels):
                        line = jnp.where(
                            picks[dy][d], 0.5 * stencil[c, d, dy * 9 + dz * 3 + dx], line
                        )
                values = values + jnp.where(bands[dz], line, 0.0)
            high = values.astype(bf16).astype(f32)
            low = values - high
            at = (dx * channels + c) * nz
            matrix[at : at + nz, :] = jnp.where(is_low, low, high).astype(bf16)

    for index, (dy, dz) in enumerate(others):
        phase_copy(index, -dy, -dz).wait_recv()
    tangent_row = slots[pl.ds(my_load, 1), :][:, TANGENT : TANGENT + 1]
    my_tangent = jnp.broadcast_to(tangent_row, (nz, nx))
    inverse_tangent = 1.0 / my_tangent
    for y in range(ny):
        second = phase_all[y] == 1
        mod = jnp.where(second, my_tangent, 1.0)
        mod_mid[y] = mod
        mod_low[y] = pltpu.roll(mod, nx - 1, 1)
        mod_high[y] = pltpu.roll(mod, 1, 1)
        mod_inv[y] = jnp.where(second, inverse_tangent, 1.0)
    ones = jnp.ones((nz, nx), f32)
    inverse_centre = [1.0 / (ones * stencil[c, c, 13]) for c in range(channels)]

    def put(buffer, y, c, value):
        both = jnp.concatenate([value, value * mod_mid[y]], axis=1)
        high = both.astype(bf16)
        low = (both - high.astype(f32)).astype(bf16)
        at = pl.multiple_of((y + 1) * slot_rows + c * nz, 16)
        spread[buffer, pl.ds(at, nz), :] = high
        spread[buffer, pl.ds(at + wide, nz), :] = high
        spread[buffer, pl.ds(at + 2 * wide, nz), :] = low

    def wrap(buffer):
        spread[buffer, 0:slot_rows, :] = spread[buffer, ny * slot_rows : (ny + 1) * slot_rows, :]
        spread[buffer, (ny + 1) * slot_rows : (ny + 2) * slot_rows, :] = spread[
            buffer, slot_rows : 2 * slot_rows, :
        ]

    for index, (dy, dz) in enumerate(others):
        force_copy(index, -dy, -dz).wait_recv()
    first_weight, weights = chebyshev_weights(SWEEPS)
    for y in range(ny):
        for c in range(channels):
            value = first_weight * (force[c, y] * inverse_centre[c])
            update[c, y] = value
            field_now[c, y] = value
            put(0, y, c, value)
    wrap(0)

    def row_product(buffer, y):
        at = y * slot_rows if isinstance(y, int) else pl.multiple_of(y * slot_rows, 16)
        return jnp.dot(
            matrix[...], spread[buffer, pl.ds(at, depth), :], preferred_element_type=f32
        )

    def finish_row(product, buffer, y, old_weight, new_weight, last):
        for c in range(channels):
            parts = []
            for dx, mod in enumerate((mod_low, mod_mid, mod_high)):
                row = (dx * channels + c) * nz
                parts.append(
                    mod[y] * product[row : row + nz, :nx] + product[row : row + nz, nx:]
                )
            stiff = parts[1] + pltpu.roll(parts[0], 1, 1) + pltpu.roll(parts[2], nx - 1, 1)
            residual = (force[c, y] - stiff * mod_inv[y]) * inverse_centre[c]
            step = old_weight * update[c, y] + new_weight * residual
            value = field_now[c, y] + step
            field_now[c, y] = value
            if not last:
                update[c, y] = step
                put(1 - buffer, y, c, value)

    def sweep_pair(pair, carry):
        for buffer in range(2):
            k = pair * 2 + buffer
            old_weight, new_weight = jnp.float32(weights[0][0]), jnp.float32(weights[0][1])
            for position in range(1, len(weights) - 1):
                old_weight = jnp.where(k == position, weights[position][0], old_weight)
                new_weight = jnp.where(k == position, weights[position][1], new_weight)
            product = row_product(buffer, 0)
            for y in range(ny):
                later = row_product(buffer, y + 1) if y + 1 < ny else None
                finish_row(product, buffer, y, old_weight, new_weight, False)
                product = later
            wrap(1 - buffer)
        return carry

    assert len(weights) % 2 == 1
    lax.fori_loop(0, (len(weights) - 1) // 2, sweep_pair, 0)

    def field_copy(dy, dz, y, load):
        to_y, to_z = turned(my_y, dy, ngy), turned(my_z, dz, ngz)
        z_at = pl.ds(pl.multiple_of(to_z * z_here, 8), z_here)
        return pltpu.make_async_remote_copy(
            src_ref=field_now.at[:, to_y * y_here + y, z_at],
            dst_ref=fields.at[0, load, :, y],
            send_sem=field_send.at[dy, dz, y], recv_sem=field_recv.at[dy, dz, y],
            device_id={"gy": to_y, "gz": to_z}, device_id_type=MESH,
        )

    final_buffer = (len(weights) - 1) % 2
    last_rows = [
        (dy, y, turned(my_y, dy, ngy) * y_here + y)
        for dy in list(range(1, ngy)) + [0]
        for y in range(y_here)
    ]
    product = row_product(final_buffer, last_rows[0][2])
    for place, (dy, y, row) in enumerate(last_rows):
        later = None
        if place + 1 < len(last_rows):
            later = row_product(final_buffer, last_rows[place + 1][2])
        finish_row(product, final_buffer, row, weights[-1][0], weights[-1][1], True)
        product = later
        for dz in list(range(1, ngz)) + [0]:
            if (dy, dz) != (0, 0):
                field_copy(dy, dz, y, my_load).start()
            else:
                for c in range(channels):
                    fields[0, my_load, c, y] = field_now[c, row, own_z, :]

    seconds = [phase[0, y] == 1 for y in range(y_here)]
    for dy, dz in mates:
        load = turned(my_y, -dy, ngy) * ngz + turned(my_z, -dz, ngz)
        if (dy, dz) != (0, 0):
            for y in range(y_here):
                field_copy(dy, dz, y, load).wait_recv()
        slope = slot_value(load, TANGENT)
        totals_of = [jnp.zeros((8, 128), f32) for _ in range(strains)]
        for y in range(y_here):
            mod = jnp.where(seconds[y], slope, 1.0)
            for c in range(channels):
                flux = mod * fields[0, load, c, y]
                for j in range(strains):
                    totals_of[j] = totals_of[j] + polar[0, c, j, y] * flux
        for j in range(strains):
            sums[j, pl.ds(load, 1), :] = jnp.sum(totals_of[j], axis=0, keepdims=True)
    ones_here = jnp.zeros((8, 128), f32)
    for y in range(y_here):
        ones_here = ones_here + jnp.where(seconds[y], 1.0, 0.0)
    second_count = jnp.sum(jnp.sum(ones_here, axis=0, keepdims=True), axis=1, keepdims=True)
    slot_table = slots[...]
    mod_sum = second_count * slot_table[:, TANGENT : TANGENT + 1] + (
        float(y_here * z_here * nx) - second_count
    )
    share = jnp.where(lane_ids < strains, slot_table * mod_sum, 0.0)
    for j in range(strains):
        share = share + jnp.where(
            lane_ids == j, jnp.sum(sums[j], axis=1, keepdims=True), 0.0
        )
    partials[len(others)] = share * (1.0 / (ny * nz * nx))

    def part_copy(index):
        return pltpu.make_async_remote_copy(
            src_ref=partials.at[len(others)], dst_ref=partials.at[index],
            send_sem=part_send.at[index], recv_sem=part_recv.at[index],
            device_id=mate_id(*others[index]), device_id_type=MESH,
        )

    for index in range(len(others)):
        part_copy(index).start()
    for index in range(len(others)):
        part_copy(index).wait_recv()
    total = partials[0]
    for index in range(1, len(mates)):
        total = total + partials[index]
    totals[my_r] = total

    def total_copy(step, owner):
        return pltpu.make_async_remote_copy(
            src_ref=totals.at[my_r], dst_ref=totals.at[owner],
            send_sem=total_send.at[step], recv_sem=total_recv.at[step],
            device_id={"rve": turned(my_r, step, groups)}, device_id_type=MESH,
        )

    for step in range(1, groups):
        total_copy(step, my_r).start()
    for step in range(1, groups):
        total_copy(step, turned(my_r, -step, groups)).wait_recv()
    mine = tables[my_r]
    answer = jnp.zeros((8, 128), f32)
    for group in range(groups):
        for rank in range(CAP):
            chosen = (mine[:, TARGET : TARGET + 1] == float(group)) & (
                mine[:, RANK : RANK + 1] == float(rank)
            )
            line = totals[group, pl.ds(my_r * CAP + rank, 1), :]
            answer = answer + jnp.where(chosen, line, 0.0)
    rows_out[...] = answer[:listed, :strains]

    for step in range(1, groups):
        table_copy(step, my_r).wait_send()
        total_copy(step, my_r).wait_send()
    for index, (dy, dz) in enumerate(others):
        phase_copy(index, 0, 0).wait_send()
        force_copy(index, 0, 0).wait_send()
        part_copy(index).wait_send()
        for y in range(y_here):
            field_copy(dy, dz, y, my_load).wait_send()


def fused_body(strain, tangent, yield_list, destination, phase_map, polarization, stencil):
    groups, ngy, ngz = (lax.axis_size(name) for name in ("rve", "gy", "gz"))
    channels = polarization.shape[1]
    strains = polarization.shape[2]
    y_here, z_here, nx = polarization.shape[3:]
    ny, nz = y_here * ngy, z_here * ngz
    loads = groups * CAP
    count = ngy * ngz
    f32 = jnp.float32
    slot_rows = 3 * channels * nz
    vmem = pl.BlockSpec(memory_space=pltpu.VMEM)
    smem = pl.BlockSpec(memory_space=pltpu.SMEM)
    cell = pltpu.VMEM((ny, nz, nx), f32)
    vector = pltpu.VMEM((channels, ny, nz, nx), f32)

    def dma(*shape):
        return pltpu.SemaphoreType.DMA(shape)

    return pl.pallas_call(
        functools.partial(kernel, groups, ngy, ngz),
        out_shape=(
            jax.ShapeDtypeStruct((1, loads, channels, y_here, z_here, nx), f32),
            jax.ShapeDtypeStruct((yield_list.shape[0], strains), f32),
        ),
        in_specs=[smem, smem, smem, smem, smem, vmem, vmem],
        out_specs=(vmem, vmem),
        scratch_shapes=[
            pltpu.VMEM((groups, 8, 128), f32),
            pltpu.VMEM((loads, 128), f32),
            pltpu.VMEM((ny, nz, nx), jnp.int32),
            pltpu.VMEM((count, channels, y_here, z_here, nx), f32),
            vector,
            pltpu.VMEM((3 * channels * nz, 3 * slot_rows), jnp.bfloat16),
            pltpu.VMEM((2, (ny + 2) * slot_rows, 2 * nx), jnp.bfloat16),
            vector,
            vector,
            cell, cell, cell, cell,
            pltpu.VMEM((strains, loads, 128), f32),
            pltpu.VMEM((count, 8, 128), f32),
            pltpu.VMEM((groups, 8, 128), f32),
            dma(groups), dma(groups), dma(count), dma(count), dma(count), dma(count),
            dma(ngy, ngz, y_here), dma(ngy, ngz, y_here),
            dma(count), dma(count), dma(groups), dma(groups),
        ],
        compiler_params=pltpu.CompilerParams(
            collective_id=0, has_side_effects=True, vmem_limit_bytes=40 * 1024 * 1024
        ),
    )(strain, tangent, yield_list, destination, stencil, phase_map, polarization)


def body_for(mesh):
    def chosen(*arguments):
        strain, _, yield_list, _, phase_map, _, _ = arguments
        loads = lax.axis_size("rve") * CAP
        one_load_each = lax.axis_size("gy") * lax.axis_size("gz") == loads
        tiled = phase_map.shape[2] == 8 and phase_map.shape[3] == 128 and loads == 8
        if one_load_each and tiled and yield_list.shape[0] <= 8:
            return fused_body(*arguments)
        return body(*arguments)

    return chosen


def solution(mesh):
    return jax.shard_map(
        body_for(mesh),
        mesh=mesh,
        in_specs=(
            P("rve", None),
            P("rve"),
            P("rve"),
            P("rve", None),
            P("rve", "gy", "gz", None),
            P("rve", None, None, "gy", "gz", None),
            P(),
        ),
        out_specs=(P("rve", None, None, "gy", "gz", None), P("rve", None)),
        check_vma=False,
    )
```

profile of v0, /device:TPU:0, one launch (start us, length us, event | category | flops | bytes accessed | tf_op | source)
XLA Modules:
  0.0 43.1 jit_solution(7892663482441387892)
XLA Ops:
  0.6 0.0 copy-start.5
  0.6 0.0 copy-start.4
  0.7 0.8 %copy.9.destination = s32[4,1]{1,0:T(4,128)S(1)} copy(s32[4,1]{0,1:T(1,128)} %param.10) | data formatting | bytes 32 | tf_op args[3]
  1.4 0.0 copy-done.5
  1.4 0.0 copy-done.4
  1.4 0.0 copy-start
  1.4 1.0 %copy-done = f32[1,3,6,4,8,128]{5,4,3,2,1,0:T(8,128)S(1)} copy-done((f32[1,3,6,4,8,128]{5,4,3,2,1,0:T(8,128)S(1)}, f32[1,3,6,4,8,128]{5,4,3,2,1,0:T(8,128)}, u32[]{:S(2)}) %copy-start) | copy-done | bytes 294936
  2.4 0.0 copy-start.1
  2.4 0.7 %copy-done.1 = s32[1,4,8,128]{3,2,1,0:T(8,128)S(1)} copy-done((s32[1,4,8,128]{3,2,1,0:T(8,128)S(1)}, s32[1,4,8,128]{3,2,1,0:T(8,128)}, u32[]{:S(2)}) %copy-start.1) | copy-done | bytes 16408
  3.1 0.0 copy-start.2
  3.1 0.7 %copy-done.2 = f32[3,3,27]{2,1,0:T(4,128)S(1)} copy-done((f32[3,3,27]{2,1,0:T(4,128)S(1)}, f32[3,3,27]{2,1,0:T(4,128)}, u32[]{:S(2)}) %copy-start.2) | copy-done | bytes 996
  3.8 0.0 copy-start.3
  3.8 0.7 %copy-done.3 = f32[8,6]{1,0:T(8,128)S(1)} copy-done((f32[8,6]{1,0:T(8,128)S(1)}, f32[8,6]{1,0:T(8,128)}, u32[]{:S(2)}) %copy-start.3) | copy-done | bytes 216
  4.5 37.3 %shard_map.86 = (f32[1,8,3,4,8,128]{5,4,3,2,1,0:T(8,128)S(1)}, f32[4,6]{1,0:T(4,128)S(1)}) custom-call(f32[8,6]{1,0:T(8,128)S(1)} %copy-done.3, f32[8]{0:T(128)S(1)} %copy-done.4, s32[4]{0:T(128)S(1)} %copy-done.5, s32[4,1]{1,0:T(4,128)S(1)} %copy.9.destination, f32[3,3,27]{2,1,0:T(4,128)S(1)} %copy-done.2, s32[1,4,8,128]{3,2,1,0:T(8,128)S(1)} %copy-done.1, ...), custom_call_target="tpu_custom_call" | custom-call | tf_op jit(solution)/shard_map/pallas_call | solution.py:518
  41.8 0.7 %copy.12 = f32[1,8,3,4,8,128]{5,4,3,2,1,0:T(8,128)} copy(f32[1,8,3,4,8,128]{5,4,3,2,1,0:T(8,128)S(1)} %get-tuple-element.4) | data formatting | bytes 786432
  42.5 0.6 %copy.13 = f32[4,6]{1,0:T(4,128)} copy(f32[4,6]{1,0:T(4,128)S(1)} %get-tuple-element.5) | data formatting | bytes 192
Async XLA Ops:
  0.6 0.8 %copy-start.5 = (s32[4]{0:T(128)S(1)}, s32[4]{0:T(128)}, u32[]{:S(2)}) copy-start(s32[4]{0:T(128)} %yield_list.1) | copy-start | bytes 52
  0.6 0.8 %copy-start.4 = (f32[8]{0:T(128)S(1)}, f32[8]{0:T(128)}, u32[]{:S(2)}) copy-start(f32[8]{0:T(128)} %tangent.1) | copy-start | bytes 100
  1.4 1.0 %copy-start = (f32[1,3,6,4,8,128]{5,4,3,2,1,0:T(8,128)S(1)}, f32[1,3,6,4,8,128]{5,4,3,2,1,0:T(8,128)}, u32[]{:S(2)}) copy-start(f32[1,3,6,4,8,128]{5,4,3,2,1,0:T(8,128)} %polar.1) | copy-start | bytes 884740
  2.4 0.7 %copy-start.1 = (s32[1,4,8,128]{3,2,1,0:T(8,128)S(1)}, s32[1,4,8,128]{3,2,1,0:T(8,128)}, u32[]{:S(2)}) copy-start(s32[1,4,8,128]{3,2,1,0:T(8,128)} %phase.1) | copy-start | bytes 49156
  3.1 0.7 %copy-start.2 = (f32[3,3,27]{2,1,0:T(4,128)S(1)}, f32[3,3,27]{2,1,0:T(4,128)}, u32[]{:S(2)}) copy-start(f32[3,3,27]{2,1,0:T(4,128)} %stencil.1) | copy-start | bytes 2920
  3.8 0.7 %copy-start.3 = (f32[8,6]{1,0:T(8,128)S(1)}, f32[8,6]{1,0:T(8,128)}, u32[]{:S(2)}) copy-start(f32[8,6]{1,0:T(8,128)} %strain.1) | copy-start | bytes 580
where the time goes:
time: 43.4 us; the launch traced here: 43.1 us
  Pallas kernels  37.3 us (86%)
  local copies, waits for them, and re-layouts  5.14 us (12%)
  between operations  0.66 us (2%)
    pallas_call x1, Pallas kernels, fused_body(): pl.pallas_call(functools.partial(kernel, groups, ngy, ngz), out_shape=(ja...  37.3 us
    unnamed x15, local copies, waits for them, and re-layouts  5.14 us

commit v1 on v0

--- a/solution.py
+++ b/solution.py
@@ -8,6 +8,7 @@
 from jax.sharding import PartitionSpec as P
 
 CAP = 2
+CORES = 2
 SWEEPS = 6
 MESH = pl.DeviceIdType.MESH
 TANGENT, TARGET, RANK, LISTED = 6, 7, 8, 9
@@ -159,17 +160,30 @@
 
 def kernel(
     groups, ngy, ngz,
-    strain, tangent, yield_list, destination, stencil, phase, polar,
+    strain_hbm, tangent_hbm, yield_hbm, destination_hbm, stencil_hbm, phase_hbm, polar_hbm,
     fields, rows_out,
-    tables, slots, phase_all, force_out, force, matrix, spread, field_now, update,
-    mod_mid, mod_low, mod_high, mod_inv, sums, partials, totals,
-    table_send, table_recv, phase_send, phase_recv, force_send, force_recv,
-    field_send, field_recv, part_send, part_recv, total_send, total_recv,
+    strain, tangent, yield_list, destination, stencil, polar, load_sem,
+    tables, slots, phase_all, polar_all, force_out, force, matrix, spread, field_now, update,
+    mod_mid, mod_low, mod_high, mod_inv, stress, totals,
+    table_send, table_recv, phase_send, phase_recv, polar_send, polar_recv,
+    relay_send, relay_recv, force_send, force_recv,
+    field_send, field_recv, total_send, total_recv, own_sem,
 ):
     f32, bf16 = jnp.float32, jnp.bfloat16
-    channels, strains = polar.shape[1], polar.shape[2]
-    y_here, z_here, nx = polar.shape[3:]
+    channels, strains = polar.shape[:2]
+    y_here, z_here, nx = polar.shape[2:]
     ny, nz = y_here * ngy, z_here * ngz
+    loaded = [
+        pltpu.make_async_copy(source, held, load_sem.at[index])
+        for index, (source, held) in enumerate(
+            [
+                (destination_hbm, destination), (yield_hbm, yield_list), (strain_hbm, strain),
+                (tangent_hbm, tangent), (polar_hbm.at[0], polar), (stencil_hbm, stencil),
+            ]
+        )
+    ]
+    for copy in loaded:
+        copy.start()
     wide = channels * nz
     slot_rows = 3 * wide
     depth = 3 * slot_rows
@@ -200,14 +214,16 @@
             barrier, inc=1, device_id={"rve": turned(my_r, step, groups)}, device_id_type=MESH
         )
 
+    for copy in loaded[:4]:
+        copy.wait()
     row_ids = lax.broadcasted_iota(jnp.int32, (8, 128), 0)
     lane_ids = lax.broadcasted_iota(jnp.int32, (8, 128), 1)
     table = jnp.zeros((8, 128), f32)
     for i in range(listed):
-        point, target = yield_list[i], destination[i, 0]
+        point, target = yield_list[i], destination[i]
         rank = jnp.int32(0)
         for k in range(i):
-            rank = rank + jnp.where(destination[k, 0] == target, 1, 0)
+            rank = rank + jnp.where(destination[k] == target, 1, 0)
         values = [strain[point, j] for j in range(strains)]
         values += [tangent[point], target.astype(f32), rank.astype(f32), jnp.float32(1.0)]
         for j, value in enumerate(values):
@@ -227,17 +243,54 @@
         y_at, z_at = block(dy, dz)
         to_y, to_z = others[index]
         return pltpu.make_async_remote_copy(
-            src_ref=phase.at[0], dst_ref=phase_all.at[y_at, z_at],
+            src_ref=phase_hbm.at[0], dst_ref=phase_all.at[y_at, z_at],
             send_sem=phase_send.at[index], recv_sem=phase_recv.at[index],
             device_id=mate_id(to_y, to_z), device_id_type=MESH,
         )
+
+    twins = [(dy, dz) for dy in range(ngy) for dz in range(0, ngz, CORES)][1:]
+    my_core = lax.rem(my_z, CORES)
+
+    def block_index(dy, dz):
+        return turned(my_y, dy, ngy) * ngz + turned(my_z, dz, ngz)
+
+    def polar_copy(index, dy, dz, c):
+        at = block_index(dy, dz)
+        return pltpu.make_async_remote_copy(
+            src_ref=polar_hbm.at[0, c], dst_ref=polar_all.at[at, c],
+            send_sem=polar_send.at[index, c], recv_sem=polar_recv.at[index, c],
+            device_id=mate_id(*twins[index]), device_id_type=MESH,
+        )
+
+    def relay_copy(index, dy, dz, c, turn):
+        at = block_index(dy, dz + turn)
+        source = polar_hbm.at[0, c] if (dy, dz) == (0, 0) else polar_all.at[at, c]
+        return pltpu.make_async_remote_copy(
+            src_ref=source, dst_ref=polar_all.at[at, c],
+            send_sem=relay_send.at[index, c], recv_sem=relay_recv.at[index, c],
+            device_id=mate_id(0, 1 - 2 * my_core), device_id_type=MESH,
+        )
+
+    def send_polar(channels_now):
+        for c in channels_now:
+            for index in range(len(twins)):
+                polar_copy(index, 0, 0, c).start()
+            relay_copy(0, 0, 0, c, 0).start()
+
+    def relay(channels_now):
+        for c in channels_now:
+            for index, (dy, dz) in enumerate(twins):
+                polar_copy(index, -dy, -dz, c).wait_recv()
+                relay_copy(index + 1, -dy, -dz, c, 0).start()
 
     for step in range(1, groups):
         table_copy(step, my_r).start()
     for index in range(len(others)):
         phase_copy(index, 0, 0).start()
     own_y, own_z = block(0, 0)
-    phase_all[own_y, own_z, :] = phase[0]
+    own_phase = pltpu.make_async_copy(phase_hbm.at[0], phase_all.at[own_y, own_z], own_sem.at[0])
+    own_phase.start()
+    send_polar(range(1))
 
     for step in range(1, groups):
         table_copy(step, turned(my_r, -step, groups)).wait_recv()
@@ -254,6 +307,8 @@
             at = source * CAP + rank
             slots[at : at + 1, :] = line
 
+    loaded[4].wait()
+
     def slot_value(load, index):
         return jnp.broadcast_to(slots[pl.ds(load, 1), :][:, index : index + 1], (8, 128))
 
@@ -270,9 +325,9 @@
         strain_of = [slot_value(load, j) for j in range(strains)]
         for c in range(channels):
             for y in range(y_here):
-                value = polar[0, c, 0, y] * strain_of[0]
+                value = polar[c, 0, y] * strain_of[0]
                 for j in range(1, strains):
-                    value = value + polar[0, c, j, y] * strain_of[j]
+                    value = value + polar[c, j, y] * strain_of[j]
                 if (dy, dz) == (0, 0):
                     force[c, my_y * y_here + y, own_z, :] = value
                 else:
@@ -280,6 +335,14 @@
         if (dy, dz) != (0, 0):
             force_copy(index, 0, 0).start()
 
+    send_polar(range(1, channels))
+    own_polar = [
+        pltpu.make_async_copy(
+            polar_hbm.at[0], polar_all.at[block_index(0, 0)], own_sem.at[1]
+        )
+    ]
+    own_polar[0].start()
+    loaded[5].wait()
     column = lax.broadcasted_iota(jnp.int32, (1, depth), 1)
     column_y = column // slot_rows
     column_kind = lax.rem(column, slot_rows) // wide
@@ -307,6 +370,7 @@
 
     for index, (dy, dz) in enumerate(others):
         phase_copy(index, -dy, -dz).wait_recv()
+    own_phase.wait()
     tangent_row = slots[pl.ds(my_load, 1), :][:, TANGENT : TANGENT + 1]
     my_tangent = jnp.broadcast_to(tangent_row, (nz, nx))
     inverse_tangent = 1.0 / my_tangent
@@ -345,6 +409,8 @@
             field_now[c, y] = value
             put(0, y, c, value)
     wrap(0)
+
+    relay(range(1))
 
     def row_product(buffer, y):
         at = y * slot_rows if isinstance(y, int) else pl.multiple_of(y * slot_rows, 16)
@@ -387,6 +453,8 @@
     assert len(weights) % 2 == 1
     lax.fori_loop(0, (len(weights) - 1) // 2, sweep_pair, 0)
 
+    relay(range(1, channels))
+
     def field_copy(dy, dz, y, load):
         to_y, to_z = turned(my_y, dy, ngy), turned(my_z, dz, ngz)
         z_at = pl.ds(pl.multiple_of(to_z * z_here, 8), z_here)
@@ -395,6 +463,12 @@
             dst_ref=fields.at[0, load, :, y],
             send_sem=field_send.at[dy, dz, y], recv_sem=field_recv.at[dy, dz, y],
             device_id={"gy": to_y, "gz": to_z}, device_id_type=MESH,
+        )
+
+    def own_field(y):
+        return pltpu.make_async_copy(
+            field_now.at[:, my_y * y_here + y, own_z], fields.at[0, my_load, :, y],
+            own_sem.at[2 + y],
         )
 
     final_buffer = (len(weights) - 1) % 2
@@ -414,67 +488,68 @@
             if (dy, dz) != (0, 0):
                 field_copy(dy, dz, y, my_load).start()
             else:
-                for c in range(channels):
-                    fields[0, my_load, c, y] = field_now[c, row, own_z, :]
-
-    seconds = [phase[0, y] == 1 for y in range(y_here)]
-    for dy, dz in mates:
-        load = turned(my_y, -dy, ngy) * ngz + turned(my_z, -dz, ngz)
-        if (dy, dz) != (0, 0):
-            for y in range(y_here):
-                field_copy(dy, dz, y, load).wait_recv()
-        slope = slot_value(load, TANGENT)
-        totals_of = [jnp.zeros((8, 128), f32) for _ in range(strains)]
-        for y in range(y_here):
-            mod = jnp.where(seconds[y], slope, 1.0)
+                own_field(y).start()
+
+    own_polar[0].wait()
+    for c in range(channels):
+        relay_copy(0, 0, 0, c, 1 - 2 * my_core).wait_recv()
+        for index, (dy, dz) in enumerate(twins):
+            relay_copy(index + 1, -dy, -dz, c, 1 - 2 * my_core).wait_recv()
+    totals_of = [jnp.zeros((z_here, nx), f32) for _ in range(strains)]
+    mod_total = jnp.zeros((z_here, nx), f32)
+    for y in range(ny):
+        for part in range(ngz):
+            z_at = slice(part * z_here, (part + 1) * z_here)
+            at = (y // y_here) * ngz + part
+            mod = mod_mid[y, z_at, :]
+            mod_total = mod_total + mod
             for c in range(channels):
-                flux = mod * fields[0, load, c, y]
+                flux = mod * field_now[c, y, z_at, :]
                 for j in range(strains):
-                    totals_of[j] = totals_of[j] + polar[0, c, j, y] * flux
-        for j in range(strains):
-            sums[j, pl.ds(load, 1), :] = jnp.sum(totals_of[j], axis=0, keepdims=True)
-    ones_here = jnp.zeros((8, 128), f32)
-    for y in range(y_here):
-        ones_here = ones_here + jnp.where(seconds[y], 1.0, 0.0)
-    second_count = jnp.sum(jnp.sum(ones_here, axis=0, keepdims=True), axis=1, keepdims=True)
-    slot_table = slots[...]
-    mod_sum = second_count * slot_table[:, TANGENT : TANGENT + 1] + (
-        float(y_here * z_here * nx) - second_count
-    )
-    share = jnp.where(lane_ids < strains, slot_table * mod_sum, 0.0)
+                    totals_of[j] = totals_of[j] + polar_all[at, c, j, y % y_here] * flux
+
+    def whole_sum(values):
+        return jnp.sum(jnp.sum(values, axis=0, keepdims=True), axis=1, keepdims=True)
+
+    line = slots[pl.ds(my_load, 1), :] * whole_sum(mod_total)
     for j in range(strains):
-        share = share + jnp.where(
-            lane_ids == j, jnp.sum(sums[j], axis=1, keepdims=True), 0.0
-        )
-    partials[len(others)] = share * (1.0 / (ny * nz * nx))
-
-    def part_copy(index):
+        line = line + jnp.where(lane_ids[:1] == j, whole_sum(totals_of[j]), 0.0)
+    stress[...] = line * (1.0 / (ny * nz * nx))
+
+    my_macro, my_rank = my_load // CAP, lax.rem(my_load, CAP)
+
+    def total_copy(dy, dz):
         return pltpu.make_async_remote_copy(
-            src_ref=partials.at[len(others)], dst_ref=partials.at[index],
-            send_sem=part_send.at[index], recv_sem=part_recv.at[index],
-            device_id=mate_id(*others[index]), device_id_type=MESH,
-        )
-
-    for index in range(len(others)):
-        part_copy(index).start()
-    for index in range(len(others)):
-        part_copy(index).wait_recv()
-    total = partials[0]
-    for index in range(1, len(mates)):
-        total = total + partials[index]
-    totals[my_r] = total
-
-    def total_copy(step, owner):
+            src_ref=stress, dst_ref=totals.at[my_r * CAP + my_rank],
+            send_sem=total_send.at[dy, dz], recv_sem=total_recv.at[my_r * CAP + my_rank],
+            device_id={"rve": my_macro, **mate_id(dy, dz)}, device_id_type=MESH,
+        )
+
+    def total_arrival(group, rank):
+        at = group * CAP + rank
         return pltpu.make_async_remote_copy(
-            src_ref=totals.at[my_r], dst_ref=totals.at[owner],
-            send_sem=total_send.at[step], recv_sem=total_recv.at[step],
-            device_id={"rve": turned(my_r, step, groups)}, device_id_type=MESH,
-        )
-
-    for step in range(1, groups):
-        total_copy(step, my_r).start()
-    for step in range(1, groups):
-        total_copy(step, turned(my_r, -step, groups)).wait_recv()
+            src_ref=stress, dst_ref=totals.at[at],
+            send_sem=total_send.at[0, 0], recv_sem=total_recv.at[at],
+            device_id={"rve": turned(my_r, 1, groups)}, device_id_type=MESH,
+        )
+
+    for dy, dz in others:
+        total_copy(dy, dz).start()
+
+    @pl.when(my_macro != my_r)
+    def _():
+        total_copy(0, 0).start()
+
+    @pl.when(my_macro == my_r)
+    def _():
+        totals[my_r * CAP + my_rank] = stress[...]
+
+    for group in range(groups):
+        for rank in range(CAP):
+            @pl.when((my_r != group) | (my_load != group * CAP + rank))
+            def _():
+                total_arrival(group, rank).wait_recv()
+
     mine = tables[my_r]
     answer = jnp.zeros((8, 128), f32)
     for group in range(groups):
@@ -482,19 +557,41 @@
             chosen = (mine[:, TARGET : TARGET + 1] == float(group)) & (
                 mine[:, RANK : RANK + 1] == float(rank)
             )
-            line = totals[group, pl.ds(my_r * CAP + rank, 1), :]
-            answer = answer + jnp.where(chosen, line, 0.0)
+            answer = answer + jnp.where(chosen, totals[group * CAP + rank], 0.0)
     rows_out[...] = answer[:listed, :strains]
 
+    @pl.when(my_macro != my_r)
+    def _():
+        total_copy(0, 0).wait_send()
+
+    for c in range(channels):
+        relay_copy(0, 0, 0, c, 0).wait_send()
+        for index, (dy, dz) in enumerate(twins):
+            polar_copy(index, 0, 0, c).wait_send()
+            relay_copy(index + 1, -dy, -dz, c, 0).wait_send()
+    for y in range(y_here):
+        own_field(y).wait()
     for step in range(1, groups):
         table_copy(step, my_r).wait_send()
-        total_copy(step, my_r).wait_send()
     for index, (dy, dz) in enumerate(others):
         phase_copy(index, 0, 0).wait_send()
         force_copy(index, 0, 0).wait_send()
-        part_copy(index).wait_send()
+        total_copy(dy, dz).wait_send()
+        load = turned(my_y, -dy, ngy) * ngz + turned(my_z, -dz, ngz)
         for y in range(y_here):
             field_copy(dy, dz, y, my_load).wait_send()
+            field_copy(dy, dz, y, load).wait_recv()
+
+
+def deliver(held_fields, held_rows, fields, rows_out, sem):
+    copies = [
+        pltpu.make_async_copy(held_fields, fields, sem.at[0]),
+        pltpu.make_async_copy(held_rows, rows_out, sem.at[1]),
+    ]
+    for copy in copies:
+        copy.start()
+    for copy in copies:
+        copy.wait()
 
 
 def fused_body(strain, tangent, yield_list, destination, phase_map, polarization, stencil):
@@ -508,25 +605,33 @@
     f32 = jnp.float32
     slot_rows = 3 * channels * nz
     vmem = pl.BlockSpec(memory_space=pltpu.VMEM)
-    smem = pl.BlockSpec(memory_space=pltpu.SMEM)
+    hbm = pl.BlockSpec(memory_space=pltpu.HBM)
     cell = pltpu.VMEM((ny, nz, nx), f32)
     vector = pltpu.VMEM((channels, ny, nz, nx), f32)
 
     def dma(*shape):
         return pltpu.SemaphoreType.DMA(shape)
 
-    return pl.pallas_call(
+    held_fields, held_rows = pl.pallas_call(
         functools.partial(kernel, groups, ngy, ngz),
         out_shape=(
             jax.ShapeDtypeStruct((1, loads, channels, y_here, z_here, nx), f32),
             jax.ShapeDtypeStruct((yield_list.shape[0], strains), f32),
         ),
-        in_specs=[smem, smem, smem, smem, smem, vmem, vmem],
+        in_specs=[hbm] * 7,
         out_specs=(vmem, vmem),
         scratch_shapes=[
+            pltpu.SMEM(strain.shape, f32),
+            pltpu.SMEM(tangent.shape, f32),
+            pltpu.SMEM(yield_list.shape, jnp.int32),
+            pltpu.SMEM(yield_list.shape, jnp.int32),
+            pltpu.SMEM(stencil.shape, f32),
+            pltpu.VMEM(polarization.shape[1:], f32),
+            dma(6),
             pltpu.VMEM((groups, 8, 128), f32),
             pltpu.VMEM((loads, 128), f32),
             pltpu.VMEM((ny, nz, nx), jnp.int32),
+            pltpu.VMEM((count, *polarization.shape[1:]), f32),
             pltpu.VMEM((count, channels, y_here, z_here, nx), f32),
             vector,
             pltpu.VMEM((3 * channels * nz, 3 * slot_rows), jnp.bfloat16),
@@ -534,17 +639,35 @@
             vector,
             vector,
             cell, cell, cell, cell,
-            pltpu.VMEM((strains, loads, 128), f32),
-            pltpu.VMEM((count, 8, 128), f32),
-            pltpu.VMEM((groups, 8, 128), f32),
-            dma(groups), dma(groups), dma(count), dma(count), dma(count), dma(count),
+            pltpu.VMEM((1, 128), f32),
+            pltpu.VMEM((loads, 1, 128), f32),
+            dma(groups), dma(groups), dma(count), dma(count),
+            dma(count // CORES, channels), dma(count // CORES, channels),
+            dma(count // CORES, channels), dma(count // CORES, channels),
+            dma(count), dma(count),
             dma(ngy, ngz, y_here), dma(ngy, ngz, y_here),
-            dma(count), dma(count), dma(groups), dma(groups),
+            dma(ngy, ngz), dma(loads), dma(2 + y_here),
         ],
         compiler_params=pltpu.CompilerParams(
             collective_id=0, has_side_effects=True, vmem_limit_bytes=40 * 1024 * 1024
         ),
-    )(strain, tangent, yield_list, destination, stencil, phase_map, polarization)
+    )(*[
+        pltpu.with_memory_space_constraint(argument, pltpu.HBM)
+        for argument in (
+            strain, tangent, yield_list, destination[:, 0], stencil, phase_map, polarization
+        )
+    ])
+    return pl.pallas_call(
+        deliver,
+        out_shape=(
+            jax.ShapeDtypeStruct(held_fields.shape, f32),
+            jax.ShapeDtypeStruct(held_rows.shape, f32),
+        ),
+        in_specs=[vmem, vmem],
+        out_specs=(hbm, hbm),
+        scratch_shapes=[dma(2)],
+        compiler_params=pltpu.CompilerParams(vmem_limit_bytes=4 * 1024 * 1024),
+    )(held_fields, held_rows)
 
 
 def body_for(mesh):

time: 43.4 us -> 35.8 us (0.82)
  local copies, waits for them, and re-layouts: 5.14 us -> 0 us
  Pallas kernels: 37.3 us -> 35 us
    unnamed x15 -> x0, local copies, waits for them, and re-layouts: 5.14 us -> none
    pallas_call x1, Pallas kernels: 37.3 us -> 34.3 us  [fused_body(): pl.pallas_call(functools.partial(kernel, groups, ngy, ngz), out_shape=(ja...]
    pallas_call x0 -> x1, Pallas kernels: none -> 0.77 us  [fused_body(): pl.pallas_call(deliver, out_shape=(jax.ShapeDtypeStruct(held_fields.shape...]
where the time goes in v1:
time: 35.8 us; the launch traced here: 35.7 us
  Pallas kernels  35 us (98%)
  between operations  0.64 us (2%)
    pallas_call x1, Pallas kernels, fused_body(): pl.pallas_call(functools.partial(kernel, groups, ngy, ngz), out_shape=(ja...  34.3 us
    pallas_call x1, Pallas kernels, fused_body(): pl.pallas_call(deliver, out_shape=(jax.ShapeDtypeStruct(held_fields.shape...  0.77 us

profile of v1, /device:TPU:0, one launch (start us, length us, event | category | flops | bytes accessed | tf_op | source)
XLA Modules:
  0.0 35.7 jit_solution(3686926588187940494)
XLA Ops:
  0.6 34.3 %shard_map.86 = (f32[1,8,3,4,8,128]{5,4,3,2,1,0:T(8,128)S(1)}, f32[4,6]{1,0:T(4,128)S(1)}) custom-call(f32[8,6]{1,0:T(8,128)} %strain_hbm.1, f32[8]{0:T(128)} %tangent_hbm.1, s32[4]{0:T(128)} %yield_hbm.1, s32[4]{0:T(128)} %bitcast.1, f32[3,3,27]{2,1,0:T(4,128)} %stencil_hbm.1, s32[1,4,8,128]{3,2,1,0:T(8,128)} %phase_hbm.1, f32[1,3,6,4,8,128]{5,4,3,2,1,0:T(8,128)} %polar_hbm.1), custom_call_target="tpu_custom_call" | custom-call | tf_op jit(solution)/shard_map/pallas_call | solution.py:615
  34.9 0.8 %shard_map.87 = (f32[1,8,3,4,8,128]{5,4,3,2,1,0:T(8,128)}, f32[4,6]{1,0:T(4,128)}) custom-call(f32[1,8,3,4,8,128]{5,4,3,2,1,0:T(8,128)S(1)} %get-tuple-element.4.held_fields, f32[4,6]{1,0:T(4,128)S(1)} %get-tuple-element.5.held_rows), custom_call_target="tpu_custom_call" | custom-call | tf_op jit(solution)/shard_map/pallas_call | solution.py:660

commit v2 on v1

--- a/solution.py
+++ b/solution.py
@@ -163,10 +163,10 @@
     strain_hbm, tangent_hbm, yield_hbm, destination_hbm, stencil_hbm, phase_hbm, polar_hbm,
     fields, rows_out,
     strain, tangent, yield_list, destination, stencil, polar, load_sem,
-    tables, slots, phase_all, polar_all, force_out, force, matrix, spread, field_now, update,
+    tables, slots, phase_all, polar_far, twin_field, force_out, force, matrix, spread, field_now, update,
     mod_mid, mod_low, mod_high, mod_inv, stress, totals,
     table_send, table_recv, phase_send, phase_recv, polar_send, polar_recv,
-    relay_send, relay_recv, force_send, force_recv,
+    twin_send, twin_recv, force_send, force_recv,
     field_send, field_recv, total_send, total_recv, own_sem,
 ):
     f32, bf16 = jnp.float32, jnp.bfloat16
@@ -248,40 +248,34 @@
             device_id=mate_id(to_y, to_z), device_id_type=MESH,
         )
 
-    twins = [(dy, dz) for dy in range(ngy) for dz in range(0, ngz, CORES)][1:]
+    across, along, corner = (1, 0), (0, CORES), (1, CORES)
+    twins = [across, along, corner]
     my_core = lax.rem(my_z, CORES)
-
-    def block_index(dy, dz):
-        return turned(my_y, dy, ngy) * ngz + turned(my_z, dz, ngz)
-
-    def polar_copy(index, dy, dz, c):
-        at = block_index(dy, dz)
-        return pltpu.make_async_remote_copy(
-            src_ref=polar_hbm.at[0, c], dst_ref=polar_all.at[at, c],
+    turn = 1 - 2 * my_core
+
+    def polar_copy(index, c):
+        return pltpu.make_async_remote_copy(
+            src_ref=polar_hbm.at[0, c], dst_ref=polar_far.at[index, c],
             send_sem=polar_send.at[index, c], recv_sem=polar_recv.at[index, c],
             device_id=mate_id(*twins[index]), device_id_type=MESH,
         )
 
-    def relay_copy(index, dy, dz, c, turn):
-        at = block_index(dy, dz + turn)
-        source = polar_hbm.at[0, c] if (dy, dz) == (0, 0) else polar_all.at[at, c]
-        return pltpu.make_async_remote_copy(
-            src_ref=source, dst_ref=polar_all.at[at, c],
-            send_sem=relay_send.at[index, c], recv_sem=relay_recv.at[index, c],
-            device_id=mate_id(0, 1 - 2 * my_core), device_id_type=MESH,
+    def onward_copy(c):
+        return pltpu.make_async_remote_copy(
+            src_ref=polar_far.at[my_core, c], dst_ref=polar_far.at[2, c],
+            send_sem=polar_send.at[2, c], recv_sem=polar_recv.at[2, c],
+            device_id=mate_id(my_core, CORES * (1 - my_core)), device_id_type=MESH,
         )
 
     def send_polar(channels_now):
         for c in channels_now:
-            for index in range(len(twins)):
-                polar_copy(index, 0, 0, c).start()
-            relay_copy(0, 0, 0, c, 0).start()
-
-    def relay(channels_now):
-        for c in channels_now:
-            for index, (dy, dz) in enumerate(twins):
-                polar_copy(index, -dy, -dz, c).wait_recv()
-                relay_copy(index + 1, -dy, -dz, c, 0).start()
+            for index in range(2):
+                polar_copy(index, c).start()
+
+    def pass_on(c):
+        for index in range(2):
+            polar_copy(index, c).wait_recv()
+        onward_copy(c).start()
 
     for step in range(1, groups):
         table_copy(step, my_r).start()
@@ -336,12 +330,6 @@
             force_copy(index, 0, 0).start()
 
     send_polar(range(1, channels))
-    own_polar = [
-        pltpu.make_async_copy(
-            polar_hbm.at[0], polar_all.at[block_index(0, 0)], own_sem.at[1]
-        )
-    ]
-    own_polar[0].start()
     loaded[5].wait()
     column = lax.broadcasted_iota(jnp.int32, (1, depth), 1)
     column_y = column // slot_rows
@@ -410,7 +398,7 @@
             put(0, y, c, value)
     wrap(0)
 
-    relay(range(1))
+    pass_on(0)
 
     def row_product(buffer, y):
         at = y * slot_rows if isinstance(y, int) else pl.multiple_of(y * slot_rows, 16)
@@ -448,21 +436,35 @@
                 finish_row(product, buffer, y, old_weight, new_weight, False)
                 product = later
             wrap(1 - buffer)
+            for c in range(channels):
+                for turn_now, passing in ((c if c else -1, pass_on),):
+                    if turn_now >= 0 and turn_now % 2 == buffer:
+                        pl.when(pair == turn_now // 2)(functools.partial(passing, c))
         return carry
 
     assert len(weights) % 2 == 1
     lax.fori_loop(0, (len(weights) - 1) // 2, sweep_pair, 0)
 
-    relay(range(1, channels))
-
-    def field_copy(dy, dz, y, load):
+    sides = [(dy, dz, dz) for dy in range(1, ngy) for dz in range(ngz)]
+    sides += [(0, 1, CORES), (0, 2, CORES + turn)]
+
+    def field_copy(dy, place, dz, y, load):
         to_y, to_z = turned(my_y, dy, ngy), turned(my_z, dz, ngz)
         z_at = pl.ds(pl.multiple_of(to_z * z_here, 8), z_here)
         return pltpu.make_async_remote_copy(
             src_ref=field_now.at[:, to_y * y_here + y, z_at],
             dst_ref=fields.at[0, load, :, y],
-            send_sem=field_send.at[dy, dz, y], recv_sem=field_recv.at[dy, dz, y],
+            send_sem=field_send.at[dy, place, y], recv_sem=field_recv.at[dy, place, y],
             device_id={"gy": to_y, "gz": to_z}, device_id_type=MESH,
+        )
+
+    def twin_copy(half, row):
+        z_at = pl.multiple_of((CORES * half + 1 - my_core) * z_here, 8)
+        return pltpu.make_async_remote_copy(
+            src_ref=field_now.at[:, row, pl.ds(z_at, z_here)],
+            dst_ref=twin_field.at[half, :, row],
+            send_sem=twin_send.at[half, row], recv_sem=twin_recv.at[half, row],
+            device_id=mate_id(0, turn), device_id_type=MESH,
         )
 
     def own_field(y):
@@ -484,52 +486,71 @@
             later = row_product(final_buffer, last_rows[place + 1][2])
         finish_row(product, final_buffer, row, weights[-1][0], weights[-1][1], True)
         product = later
-        for dz in list(range(1, ngz)) + [0]:
-            if (dy, dz) != (0, 0):
-                field_copy(dy, dz, y, my_load).start()
-            else:
-                own_field(y).start()
-
-    own_polar[0].wait()
-    for c in range(channels):
-        relay_copy(0, 0, 0, c, 1 - 2 * my_core).wait_recv()
-        for index, (dy, dz) in enumerate(twins):
-            relay_copy(index + 1, -dy, -dz, c, 1 - 2 * my_core).wait_recv()
-    totals_of = [jnp.zeros((z_here, nx), f32) for _ in range(strains)]
-    mod_total = jnp.zeros((z_here, nx), f32)
-    for y in range(ny):
-        for part in range(ngz):
-            z_at = slice(part * z_here, (part + 1) * z_here)
-            at = (y // y_here) * ngz + part
-            mod = mod_mid[y, z_at, :]
-            mod_total = mod_total + mod
+        for half in range(ngz // CORES):
+            twin_copy(half, row).start()
+        for side, where, dz in sides:
+            if side == dy:
+                field_copy(dy, where, dz, y, my_load).start()
+        if dy == 0:
+            own_field(y).start()
+
+    for row in range(ny):
+        for half in range(ngz // CORES):
+            twin_copy(half, row).wait_recv()
+    for c in range(1, channels + 1):
+        if c < channels:
+            polar_copy(2, c).wait_recv()
+        else:
+            polar_copy(2, 0).wait_recv()
+    twin_load = my_load + turn
+    slopes = [slot_value(my_load, TANGENT), slot_value(twin_load, TANGENT)]
+    totals_of = [[jnp.zeros((z_here, nx), f32) for _ in range(strains)] for _ in range(2)]
+    counted = jnp.zeros((z_here, nx), f32)
+    for index, (dy, dz) in enumerate([(0, 0)] + twins):
+        part = lax.rem(my_z // CORES + dz // CORES, ngz // CORES)
+        for y in range(y_here):
+            row = turned(my_y, dy, ngy) * y_here + y
+            z_at = pl.ds(pl.multiple_of((CORES * part + my_core) * z_here, 8), z_here)
+            second = phase_all[row, z_at, :] == 1
+            counted = counted + jnp.where(second, 1.0, 0.0)
+            mods = [jnp.where(second, slope, 1.0) for slope in slopes]
             for c in range(channels):
-                flux = mod * field_now[c, y, z_at, :]
+                theirs = twin_field[part, c, row]
+                if index == 0:
+                    fields[0, twin_load, c, y] = theirs
+                fluxes = [mods[0] * field_now[c, row, z_at, :], mods[1] * theirs]
                 for j in range(strains):
-                    totals_of[j] = totals_of[j] + polar_all[at, c, j, y % y_here] * flux
+                    weight = polar[c, j, y] if index == 0 else polar_far[index - 1, c, j, y]
+                    for which in range(2):
+                        totals_of[which][j] = totals_of[which][j] + weight * fluxes[which]
 
     def whole_sum(values):
         return jnp.sum(jnp.sum(values, axis=0, keepdims=True), axis=1, keepdims=True)
 
-    line = slots[pl.ds(my_load, 1), :] * whole_sum(mod_total)
-    for j in range(strains):
-        line = line + jnp.where(lane_ids[:1] == j, whole_sum(totals_of[j]), 0.0)
-    stress[...] = line * (1.0 / (ny * nz * nx))
-
-    my_macro, my_rank = my_load // CAP, lax.rem(my_load, CAP)
+    second_count = whole_sum(counted)
+    for which, load in enumerate((my_load, twin_load)):
+        line = slots[pl.ds(load, 1), :]
+        mod_sum = second_count * line[:, TANGENT : TANGENT + 1] + (
+            float(len(twins) + 1) * y_here * z_here * nx - second_count
+        )
+        line = line * mod_sum
+        for j in range(strains):
+            line = line + jnp.where(lane_ids[:1] == j, whole_sum(totals_of[which][j]), 0.0)
+        stress[lax.rem(load, CAP)] = line * (1.0 / (ny * nz * nx))
+
+    my_macro = my_load // CAP
 
     def total_copy(dy, dz):
         return pltpu.make_async_remote_copy(
-            src_ref=stress, dst_ref=totals.at[my_r * CAP + my_rank],
-            send_sem=total_send.at[dy, dz], recv_sem=total_recv.at[my_r * CAP + my_rank],
+            src_ref=stress, dst_ref=totals.at[my_r, my_core],
+            send_sem=total_send.at[dy, dz], recv_sem=total_recv.at[my_r, my_core],
             device_id={"rve": my_macro, **mate_id(dy, dz)}, device_id_type=MESH,
         )
 
-    def total_arrival(group, rank):
-        at = group * CAP + rank
-        return pltpu.make_async_remote_copy(
-            src_ref=stress, dst_ref=totals.at[at],
-            send_sem=total_send.at[0, 0], recv_sem=total_recv.at[at],
+    def total_arrival(group, core):
+        return pltpu.make_async_remote_copy(
+            src_ref=stress, dst_ref=totals.at[group, core],
+            send_sem=total_send.at[0, 0], recv_sem=total_recv.at[group, core],
             device_id={"rve": turned(my_r, 1, groups)}, device_id_type=MESH,
         )
 
@@ -542,13 +563,13 @@
 
     @pl.when(my_macro == my_r)
     def _():
-        totals[my_r * CAP + my_rank] = stress[...]
+        totals[my_r, my_core] = stress[...]
 
     for group in range(groups):
-        for rank in range(CAP):
-            @pl.when((my_r != group) | (my_load != group * CAP + rank))
+        for core in range(CORES):
+            @pl.when((my_r != group) | (my_macro != group) | (my_core != core))
             def _():
-                total_arrival(group, rank).wait_recv()
+                total_arrival(group, core).wait_recv()
 
     mine = tables[my_r]
     answer = jnp.zeros((8, 128), f32)
@@ -557,7 +578,10 @@
             chosen = (mine[:, TARGET : TARGET + 1] == float(group)) & (
                 mine[:, RANK : RANK + 1] == float(rank)
             )
-            answer = answer + jnp.where(chosen, totals[group * CAP + rank], 0.0)
+            line = totals[group, 0, rank]
+            for core in range(1, CORES):
+                line = line + totals[group, core, rank]
+            answer = answer + jnp.where(chosen, line, 0.0)
     rows_out[...] = answer[:listed, :strains]
 
     @pl.when(my_macro != my_r)
@@ -565,10 +589,9 @@
         total_copy(0, 0).wait_send()
 
     for c in range(channels):
-        relay_copy(0, 0, 0, c, 0).wait_send()
-        for index, (dy, dz) in enumerate(twins):
-            polar_copy(index, 0, 0, c).wait_send()
-            relay_copy(index + 1, -dy, -dz, c, 0).wait_send()
+        for index in range(2):
+            polar_copy(index, c).wait_send()
+        onward_copy(c).wait_send()
     for y in range(y_here):
         own_field(y).wait()
     for step in range(1, groups):
@@ -577,10 +600,14 @@
         phase_copy(index, 0, 0).wait_send()
         force_copy(index, 0, 0).wait_send()
         total_copy(dy, dz).wait_send()
+    for dy, where, dz in sides:
         load = turned(my_y, -dy, ngy) * ngz + turned(my_z, -dz, ngz)
         for y in range(y_here):
-            field_copy(dy, dz, y, my_load).wait_send()
-            field_copy(dy, dz, y, load).wait_recv()
+            field_copy(dy, where, dz, y, my_load).wait_send()
+            field_copy(dy, where, dz, y, load).wait_recv()
+    for row in range(ny):
+        for half in range(ngz // CORES):
+            twin_copy(half, row).wait_send()
 
 
 def deliver(held_fields, held_rows, fields, rows_out, sem):
@@ -631,7 +658,8 @@
             pltpu.VMEM((groups, 8, 128), f32),
             pltpu.VMEM((loads, 128), f32),
             pltpu.VMEM((ny, nz, nx), jnp.int32),
-            pltpu.VMEM((count, *polarization.shape[1:]), f32),
+            pltpu.VMEM((3, *polarization.shape[1:]), f32),
+            pltpu.VMEM((ngz // CORES, channels, ny, z_here, nx), f32),
             pltpu.VMEM((count, channels, y_here, z_here, nx), f32),
             vector,
             pltpu.VMEM((3 * channels * nz, 3 * slot_rows), jnp.bfloat16),
@@ -639,14 +667,14 @@
             vector,
             vector,
             cell, cell, cell, cell,
-            pltpu.VMEM((1, 128), f32),
-            pltpu.VMEM((loads, 1, 128), f32),
+            pltpu.VMEM((CAP, 1, 128), f32),
+            pltpu.VMEM((groups, CORES, CAP, 1, 128), f32),
             dma(groups), dma(groups), dma(count), dma(count),
-            dma(count // CORES, channels), dma(count // CORES, channels),
-            dma(count // CORES, channels), dma(count // CORES, channels),
+            dma(3, channels), dma(3, channels),
+            dma(ngz // CORES, ny), dma(ngz // CORES, ny),
             dma(count), dma(count),
             dma(ngy, ngz, y_here), dma(ngy, ngz, y_here),
-            dma(ngy, ngz), dma(loads), dma(2 + y_here),
+            dma(ngy, ngz), dma(groups, CORES), dma(2 + y_here),
         ],
         compiler_params=pltpu.CompilerParams(
             collective_id=0, has_side_effects=True, vmem_limit_bytes=40 * 1024 * 1024
@@ -674,7 +702,7 @@
     def chosen(*arguments):
         strain, _, yield_list, _, phase_map, _, _ = arguments
         loads = lax.axis_size("rve") * CAP
-        one_load_each = lax.axis_size("gy") * lax.axis_size("gz") == loads
+        one_load_each = lax.axis_size("gy") == 2 and lax.axis_size("gz") == 2 * CORES
         tiled = phase_map.shape[2] == 8 and phase_map.shape[3] == 128 and loads == 8
         if one_load_each and tiled and yield_list.shape[0] <= 8:
             return fused_body(*arguments)

time: 35.8 us -> 33.4 us (0.933)
  Pallas kernels: 35 us -> 32.6 us
    pallas_call x1, Pallas kernels: 34.3 us -> 31.9 us  [fused_body(): pl.pallas_call(functools.partial(kernel, groups, ngy, ngz), out_shape=(ja...]
where the time goes in v2:
time: 33.4 us; the launch traced here: 33.3 us
  Pallas kernels  32.6 us (98%)
  between operations  0.64 us (2%)
    pallas_call x1, Pallas kernels, fused_body(): pl.pallas_call(functools.partial(kernel, groups, ngy, ngz), out_shape=(ja...  31.9 us
    pallas_call x1, Pallas kernels, fused_body(): pl.pallas_call(deliver, out_shape=(jax.ShapeDtypeStruct(held_fields.shape...  0.77 us

profile of v2, /device:TPU:0, one launch (start us, length us, event | category | flops | bytes accessed | tf_op | source)
XLA Modules:
  0.0 33.3 jit_solution(5924039203661126741)
XLA Ops:
  0.6 31.9 %shard_map.86 = (f32[1,8,3,4,8,128]{5,4,3,2,1,0:T(8,128)S(1)}, f32[4,6]{1,0:T(4,128)S(1)}) custom-call(f32[8,6]{1,0:T(8,128)} %strain_hbm.1, f32[8]{0:T(128)} %tangent_hbm.1, s32[4]{0:T(128)} %yield_hbm.1, s32[4]{0:T(128)} %bitcast.1, f32[3,3,27]{2,1,0:T(4,128)} %stencil_hbm.1, s32[1,4,8,128]{3,2,1,0:T(8,128)} %phase_hbm.1, f32[1,3,6,4,8,128]{5,4,3,2,1,0:T(8,128)} %polar_hbm.1), custom_call_target="tpu_custom_call" | custom-call | tf_op jit(solution)/shard_map/pallas_call | solution.py:642
  32.5 0.8 %shard_map.87 = (f32[1,8,3,4,8,128]{5,4,3,2,1,0:T(8,128)}, f32[4,6]{1,0:T(4,128)}) custom-call(f32[1,8,3,4,8,128]{5,4,3,2,1,0:T(8,128)S(1)} %get-tuple-element.4.held_fields, f32[4,6]{1,0:T(4,128)S(1)} %get-tuple-element.5.held_rows), custom_call_target="tpu_custom_call" | custom-call | tf_op jit(solution)/shard_map/pallas_call | solution.py:688

commit v3 on v2

--- a/solution.py
+++ b/solution.py
@@ -9,6 +9,9 @@
 
 CAP = 2
 CORES = 2
+SKEWED = 1
+PASSES = (16, 24)
+SENT_ROWS = 2
 SWEEPS = 6
 MESH = pl.DeviceIdType.MESH
 TANGENT, TARGET, RANK, LISTED = 6, 7, 8, 9
@@ -44,6 +47,34 @@
         weights.append((rho_after * rho_before, 2.0 * rho_after / half_width))
         rho_before = rho_after
     return (1.0 / centre_value, weights)
+
+
+def skewed_order(rows, half, levels):
+    def needed(level, row):
+        steps = [(level, row)]
+        if level:
+            for shift in (-1, 0, 1):
+                steps += needed(level - 1, (row + shift) % rows)
+        return steps
+
+    finals = []
+    for away in range(rows // 2):
+        finals += [(half + away) % rows, (half - 1 - away) % rows]
+    finals = [row for pair in range(0, rows, 4) for row in finals[pair : pair + 4 : 2] + finals[pair + 1 : pair + 4 : 2]]
+    placed = {}
+    order = []
+    while len(order) < rows * levels:
+        choice = None
+        for lag in (2, 1):
+            for final in finals:
+                for level, row in sorted(set(needed(levels - 1, final))):
+                    inputs = needed(level, row)[1:]
+                    ready = all(placed.get(step, rows * levels) <= len(order) - lag for step in inputs)
+                    if choice is None and (level, row) not in placed and ready:
+                        choice = (level, row)
+        placed[choice] = len(order)
+        order.append(choice)
+    return order
 
 
 def trim_margin(values_in, margin_have, margin_want, first_dim):
@@ -201,9 +232,9 @@
     def mate_id(dy, dz):
         return {"gy": turned(my_y, dy, ngy), "gz": turned(my_z, dz, ngz)}
 
-    def block(dy, dz):
-        y_at = turned(my_y, dy, ngy) * y_here
-        z_at = pl.multiple_of(turned(my_z, dz, ngz) * z_here, 8)
+    def block(dy):
+        y_at = -dy % ngy * y_here
+        z_at = pl.multiple_of(my_z * z_here, 8)
         return pl.ds(y_at, y_here), pl.ds(z_at, z_here)
 
     barrier = pltpu.get_barrier_semaphore()
@@ -239,9 +270,9 @@
             device_id={"rve": turned(my_r, step, groups)}, device_id_type=MESH,
         )
 
-    def phase_copy(index, dy, dz):
-        y_at, z_at = block(dy, dz)
+    def phase_copy(index):
         to_y, to_z = others[index]
+        y_at, z_at = block(to_y)
         return pltpu.make_async_remote_copy(
             src_ref=phase_hbm.at[0], dst_ref=phase_all.at[y_at, z_at],
             send_sem=phase_send.at[index], recv_sem=phase_recv.at[index],
@@ -280,8 +311,8 @@
     for step in range(1, groups):
         table_copy(step, my_r).start()
     for index in range(len(others)):
-        phase_copy(index, 0, 0).start()
-    own_y, own_z = block(0, 0)
+        phase_copy(index).start()
+    own_y, own_z = block(0)
     own_phase = pltpu.make_async_copy(phase_hbm.at[0], phase_all.at[own_y, own_z], own_sem.at[0])
     own_phase.start()
     send_polar(range(1))
@@ -306,8 +337,8 @@
     def slot_value(load, index):
         return jnp.broadcast_to(slots[pl.ds(load, 1), :][:, index : index + 1], (8, 128))
 
-    def force_copy(index, dy, dz):
-        y_at, z_at = block(dy, dz)
+    def force_copy(index):
+        y_at, z_at = block(others[index][0])
         return pltpu.make_async_remote_copy(
             src_ref=force_out.at[index], dst_ref=force.at[:, y_at, z_at],
             send_sem=force_send.at[index], recv_sem=force_recv.at[index],
@@ -323,11 +354,11 @@
                 for j in range(1, strains):
                     value = value + polar[c, j, y] * strain_of[j]
                 if (dy, dz) == (0, 0):
-                    force[c, my_y * y_here + y, own_z, :] = value
+                    force[c, y, own_z, :] = value
                 else:
                     force_out[index, c, y] = value
         if (dy, dz) != (0, 0):
-            force_copy(index, 0, 0).start()
+            force_copy(index).start()
 
     send_polar(range(1, channels))
     loaded[5].wait()
@@ -357,7 +388,7 @@
             matrix[at : at + nz, :] = jnp.where(is_low, low, high).astype(bf16)
 
     for index, (dy, dz) in enumerate(others):
-        phase_copy(index, -dy, -dz).wait_recv()
+        phase_copy(index).wait_recv()
     own_phase.wait()
     tangent_row = slots[pl.ds(my_load, 1), :][:, TANGENT : TANGENT + 1]
     my_tangent = jnp.broadcast_to(tangent_row, (nz, nx))
@@ -376,32 +407,30 @@
         both = jnp.concatenate([value, value * mod_mid[y]], axis=1)
         high = both.astype(bf16)
         low = (both - high.astype(f32)).astype(bf16)
-        at = pl.multiple_of((y + 1) * slot_rows + c * nz, 16)
-        spread[buffer, pl.ds(at, nz), :] = high
-        spread[buffer, pl.ds(at + wide, nz), :] = high
-        spread[buffer, pl.ds(at + 2 * wide, nz), :] = low
-
-    def wrap(buffer):
-        spread[buffer, 0:slot_rows, :] = spread[buffer, ny * slot_rows : (ny + 1) * slot_rows, :]
-        spread[buffer, (ny + 1) * slot_rows : (ny + 2) * slot_rows, :] = spread[
-            buffer, slot_rows : 2 * slot_rows, :
-        ]
-
-    for index, (dy, dz) in enumerate(others):
-        force_copy(index, -dy, -dz).wait_recv()
+        places = [y + 1] + ([ny + 1] if y == 0 else []) + ([0] if y == ny - 1 else [])
+        for place in places:
+            at = place * slot_rows + c * nz
+            spread[buffer, at : at + nz, :] = high
+            spread[buffer, at + wide : at + wide + nz, :] = high
+            spread[buffer, at + 2 * wide : at + 2 * wide + nz, :] = low
+
     first_weight, weights = chebyshev_weights(SWEEPS)
-    for y in range(ny):
+    quarters = (ngz // CORES, CORES, z_here, nx)
+    for y in list(range(y_here, ny)) + list(range(y_here)):
+        if y % y_here == 0:
+            for index, (dy, dz) in enumerate(others):
+                if dy == y // y_here:
+                    force_copy(index).wait_recv()
         for c in range(channels):
             value = first_weight * (force[c, y] * inverse_centre[c])
             update[c, y] = value
-            field_now[c, y] = value
+            field_now[c, y] = value.reshape(quarters)
             put(0, y, c, value)
-    wrap(0)
 
     pass_on(0)
 
     def row_product(buffer, y):
-        at = y * slot_rows if isinstance(y, int) else pl.multiple_of(y * slot_rows, 16)
+        at = y * slot_rows
         return jnp.dot(
             matrix[...], spread[buffer, pl.ds(at, depth), :], preferred_element_type=f32
         )
@@ -417,86 +446,91 @@
             stiff = parts[1] + pltpu.roll(parts[0], 1, 1) + pltpu.roll(parts[2], nx - 1, 1)
             residual = (force[c, y] - stiff * mod_inv[y]) * inverse_centre[c]
             step = old_weight * update[c, y] + new_weight * residual
-            value = field_now[c, y] + step
-            field_now[c, y] = value
+            value = field_now[c, y].reshape(nz, nx) + step
+            field_now[c, y] = value.reshape(quarters)
             if not last:
                 update[c, y] = step
                 put(1 - buffer, y, c, value)
 
-    def sweep_pair(pair, carry):
-        for buffer in range(2):
-            k = pair * 2 + buffer
-            old_weight, new_weight = jnp.float32(weights[0][0]), jnp.float32(weights[0][1])
-            for position in range(1, len(weights) - 1):
-                old_weight = jnp.where(k == position, weights[position][0], old_weight)
-                new_weight = jnp.where(k == position, weights[position][1], new_weight)
-            product = row_product(buffer, 0)
-            for y in range(ny):
-                later = row_product(buffer, y + 1) if y + 1 < ny else None
-                finish_row(product, buffer, y, old_weight, new_weight, False)
-                product = later
-            wrap(1 - buffer)
-            for c in range(channels):
-                for turn_now, passing in ((c if c else -1, pass_on),):
-                    if turn_now >= 0 and turn_now % 2 == buffer:
-                        pl.when(pair == turn_now // 2)(functools.partial(passing, c))
+    def sweep(k, carry):
+        old_weight, new_weight = jnp.float32(weights[0][0]), jnp.float32(weights[0][1])
+        for position in range(1, plain):
+            old_weight = jnp.where(k == position, weights[position][0], old_weight)
+            new_weight = jnp.where(k == position, weights[position][1], new_weight)
+        buffer = lax.rem(k, 2)
+        product = row_product(buffer, 0)
+        for y in range(ny):
+            later = row_product(buffer, y + 1) if y + 1 < ny else None
+            finish_row(product, buffer, y, old_weight, new_weight, False)
+            product = later
+        for c, after in enumerate(PASSES):
+            if after % ny == 0 and after <= plain * ny:
+                pl.when(k == after // ny - 1)(functools.partial(pass_on, c + 1))
         return carry
 
-    assert len(weights) % 2 == 1
-    lax.fori_loop(0, (len(weights) - 1) // 2, sweep_pair, 0)
+    plain = len(weights) - SKEWED
+    lax.fori_loop(0, plain, sweep, 0)
 
     sides = [(dy, dz, dz) for dy in range(1, ngy) for dz in range(ngz)]
     sides += [(0, 1, CORES), (0, 2, CORES + turn)]
 
-    def field_copy(dy, place, dz, y, load):
+    groups_here = y_here // SENT_ROWS
+
+    def rows_of(group):
+        return pl.ds(group * SENT_ROWS, SENT_ROWS)
+
+    def field_copy(dy, place, dz, group, load):
         to_y, to_z = turned(my_y, dy, ngy), turned(my_z, dz, ngz)
-        z_at = pl.ds(pl.multiple_of(to_z * z_here, 8), z_here)
-        return pltpu.make_async_remote_copy(
-            src_ref=field_now.at[:, to_y * y_here + y, z_at],
-            dst_ref=fields.at[0, load, :, y],
-            send_sem=field_send.at[dy, place, y], recv_sem=field_recv.at[dy, place, y],
+        return pltpu.make_async_remote_copy(
+            src_ref=field_now.at[
+                :, rows_of(dy * groups_here + group), to_z // CORES, lax.rem(to_z, CORES)
+            ],
+            dst_ref=fields.at[0, load, :, rows_of(group)],
+            send_sem=field_send.at[dy, place, group], recv_sem=field_recv.at[dy, place, group],
             device_id={"gy": to_y, "gz": to_z}, device_id_type=MESH,
         )
 
-    def twin_copy(half, row):
-        z_at = pl.multiple_of((CORES * half + 1 - my_core) * z_here, 8)
-        return pltpu.make_async_remote_copy(
-            src_ref=field_now.at[:, row, pl.ds(z_at, z_here)],
-            dst_ref=twin_field.at[half, :, row],
-            send_sem=twin_send.at[half, row], recv_sem=twin_recv.at[half, row],
+    def twin_copy(group):
+        return pltpu.make_async_remote_copy(
+            src_ref=field_now.at[:, rows_of(group), :, 1 - my_core],
+            dst_ref=twin_field.at[:, rows_of(group)],
+            send_sem=twin_send.at[group], recv_sem=twin_recv.at[group],
             device_id=mate_id(0, turn), device_id_type=MESH,
         )
 
-    def own_field(y):
+    def own_field(group):
         return pltpu.make_async_copy(
-            field_now.at[:, my_y * y_here + y, own_z], fields.at[0, my_load, :, y],
-            own_sem.at[2 + y],
-        )
-
-    final_buffer = (len(weights) - 1) % 2
-    last_rows = [
-        (dy, y, turned(my_y, dy, ngy) * y_here + y)
-        for dy in list(range(1, ngy)) + [0]
-        for y in range(y_here)
-    ]
-    product = row_product(final_buffer, last_rows[0][2])
-    for place, (dy, y, row) in enumerate(last_rows):
+            field_now.at[:, rows_of(group), my_z // CORES, my_core],
+            fields.at[0, my_load, :, rows_of(group)],
+            own_sem.at[2 + group],
+        )
+
+    order = skewed_order(ny, y_here, SKEWED)
+    product = row_product(plain % 2, order[0][1])
+    for place, (level, row) in enumerate(order):
         later = None
-        if place + 1 < len(last_rows):
-            later = row_product(final_buffer, last_rows[place + 1][2])
-        finish_row(product, final_buffer, row, weights[-1][0], weights[-1][1], True)
+        if place + 1 < len(order):
+            later = row_product((plain + order[place + 1][0]) % 2, order[place + 1][1])
+        last = level == SKEWED - 1
+        finish_row(product, (plain + level) % 2, row, *weights[plain + level], last)
         product = later
-        for half in range(ngz // CORES):
-            twin_copy(half, row).start()
-        for side, where, dz in sides:
-            if side == dy:
-                field_copy(dy, where, dz, y, my_load).start()
-        if dy == 0:
-            own_field(y).start()
-
-    for row in range(ny):
-        for half in range(ngz // CORES):
-            twin_copy(half, row).wait_recv()
+        group = row // SENT_ROWS
+        waiting = [step for step in order[place + 1 :] if step in [
+            (SKEWED - 1, group * SENT_ROWS + other) for other in range(SENT_ROWS)
+        ]]
+        if last and not waiting:
+            twin_copy(group).start()
+            for side, where, dz in sides:
+                if side == group // groups_here:
+                    field_copy(side, where, dz, group % groups_here, my_load).start()
+            if group < groups_here:
+                own_field(group).start()
+        for c, after in enumerate(PASSES):
+            if after == plain * ny + place + 1 and after > plain * ny:
+                pass_on(c + 1)
+
+    for group in range(ngy * groups_here):
+        twin_copy(group).wait_recv()
     for c in range(1, channels + 1):
         if c < channels:
             polar_copy(2, c).wait_recv()
@@ -509,16 +543,16 @@
     for index, (dy, dz) in enumerate([(0, 0)] + twins):
         part = lax.rem(my_z // CORES + dz // CORES, ngz // CORES)
         for y in range(y_here):
-            row = turned(my_y, dy, ngy) * y_here + y
+            row = dy * y_here + y
             z_at = pl.ds(pl.multiple_of((CORES * part + my_core) * z_here, 8), z_here)
             second = phase_all[row, z_at, :] == 1
             counted = counted + jnp.where(second, 1.0, 0.0)
             mods = [jnp.where(second, slope, 1.0) for slope in slopes]
             for c in range(channels):
-                theirs = twin_field[part, c, row]
+                theirs = twin_field[c, row, part]
                 if index == 0:
                     fields[0, twin_load, c, y] = theirs
-                fluxes = [mods[0] * field_now[c, row, z_at, :], mods[1] * theirs]
+                fluxes = [mods[0] * field_now[c, row, part, my_core], mods[1] * theirs]
                 for j in range(strains):
                     weight = polar[c, j, y] if index == 0 else polar_far[index - 1, c, j, y]
                     for which in range(2):
@@ -592,22 +626,21 @@
         for index in range(2):
             polar_copy(index, c).wait_send()
         onward_copy(c).wait_send()
-    for y in range(y_here):
-        own_field(y).wait()
+    for group in range(groups_here):
+        own_field(group).wait()
     for step in range(1, groups):
         table_copy(step, my_r).wait_send()
     for index, (dy, dz) in enumerate(others):
-        phase_copy(index, 0, 0).wait_send()
-        force_copy(index, 0, 0).wait_send()
+        phase_copy(index).wait_send()
+        force_copy(index).wait_send()
         total_copy(dy, dz).wait_send()
     for dy, where, dz in sides:
         load = turned(my_y, -dy, ngy) * ngz + turned(my_z, -dz, ngz)
-        for y in range(y_here):
-            field_copy(dy, where, dz, y, my_load).wait_send()
-            field_copy(dy, where, dz, y, load).wait_recv()
-    for row in range(ny):
-        for half in range(ngz // CORES):
-            twin_copy(half, row).wait_send()
+        for group in range(groups_here):
+            field_copy(dy, where, dz, group, my_load).wait_send()
+            field_copy(dy, where, dz, group, load).wait_recv()
+    for group in range(ngy * groups_here):
+        twin_copy(group).wait_send()
 
 
 def deliver(held_fields, held_rows, fields, rows_out, sem):
@@ -659,19 +692,19 @@
             pltpu.VMEM((loads, 128), f32),
             pltpu.VMEM((ny, nz, nx), jnp.int32),
             pltpu.VMEM((3, *polarization.shape[1:]), f32),
-            pltpu.VMEM((ngz // CORES, channels, ny, z_here, nx), f32),
+            pltpu.VMEM((channels, ny, ngz // CORES, z_here, nx), f32),
             pltpu.VMEM((count, channels, y_here, z_here, nx), f32),
             vector,
             pltpu.VMEM((3 * channels * nz, 3 * slot_rows), jnp.bfloat16),
             pltpu.VMEM((2, (ny + 2) * slot_rows, 2 * nx), jnp.bfloat16),
-            vector,
+            pltpu.VMEM((channels, ny, ngz // CORES, CORES, z_here, nx), f32),
             vector,
             cell, cell, cell, cell,
             pltpu.VMEM((CAP, 1, 128), f32),
             pltpu.VMEM((groups, CORES, CAP, 1, 128), f32),
             dma(groups), dma(groups), dma(count), dma(count),
             dma(3, channels), dma(3, channels),
-            dma(ngz // CORES, ny), dma(ngz // CORES, ny),
+            dma(ny), dma(ny),
             dma(count), dma(count),
             dma(ngy, ngz, y_here), dma(ngy, ngz, y_here),
             dma(ngy, ngz), dma(groups, CORES), dma(2 + y_here),

time: 33.4 us -> 32.6 us (0.976)
  Pallas kernels: 32.6 us -> 31.9 us
    pallas_call x1, Pallas kernels: 31.9 us -> 31.1 us  [fused_body(): pl.pallas_call(functools.partial(kernel, groups, ngy, ngz), out_shape=(ja...]
where the time goes in v3:
time: 32.6 us; the launch traced here: 32.5 us
  Pallas kernels  31.9 us (98%)
  between operations  0.64 us (2%)
    pallas_call x1, Pallas kernels, fused_body(): pl.pallas_call(functools.partial(kernel, groups, ngy, ngz), out_shape=(ja...  31.1 us
    pallas_call x1, Pallas kernels, fused_body(): pl.pallas_call(deliver, out_shape=(jax.ShapeDtypeStruct(held_fields.shape...  0.77 us

profile of v3, /device:TPU:0, one launch (start us, length us, event | category | flops | bytes accessed | tf_op | source)
XLA Modules:
  0.0 32.5 jit_solution(13946223660045417734)
XLA Ops:
  0.6 31.1 %shard_map.86 = (f32[1,8,3,4,8,128]{5,4,3,2,1,0:T(8,128)S(1)}, f32[4,6]{1,0:T(4,128)S(1)}) custom-call(f32[8,6]{1,0:T(8,128)} %strain_hbm.1, f32[8]{0:T(128)} %tangent_hbm.1, s32[4]{0:T(128)} %yield_hbm.1, s32[4]{0:T(128)} %bitcast.1, f32[3,3,27]{2,1,0:T(4,128)} %stencil_hbm.1, s32[1,4,8,128]{3,2,1,0:T(8,128)} %phase_hbm.1, f32[1,3,6,4,8,128]{5,4,3,2,1,0:T(8,128)} %polar_hbm.1), custom_call_target="tpu_custom_call" | custom-call | tf_op jit(solution)/shard_map/pallas_call | solution.py:675
  31.7 0.8 %shard_map.87 = (f32[1,8,3,4,8,128]{5,4,3,2,1,0:T(8,128)}, f32[4,6]{1,0:T(4,128)}) custom-call(f32[1,8,3,4,8,128]{5,4,3,2,1,0:T(8,128)S(1)} %get-tuple-element.4.held_fields, f32[4,6]{1,0:T(4,128)S(1)} %get-tuple-element.5.held_rows), custom_call_target="tpu_custom_call" | custom-call | tf_op jit(solution)/shard_map/pallas_call | solution.py:721

commit v4 on v3

--- a/solution.py
+++ b/solution.py
@@ -213,8 +213,6 @@
             ]
         )
     ]
-    for copy in loaded:
-        copy.start()
     wide = channels * nz
     slot_rows = 3 * wide
     depth = 3 * slot_rows
@@ -238,13 +236,16 @@
         return pl.ds(y_at, y_here), pl.ds(z_at, z_here)
 
     barrier = pltpu.get_barrier_semaphore()
-    for dy, dz in others:
-        pl.semaphore_signal(barrier, inc=1, device_id=mate_id(dy, dz), device_id_type=MESH)
     for step in range(1, groups):
         pl.semaphore_signal(
             barrier, inc=1, device_id={"rve": turned(my_r, step, groups)}, device_id_type=MESH
         )
-
+    for copy in loaded[:4]:
+        copy.start()
+    for dy, dz in others:
+        pl.semaphore_signal(barrier, inc=1, device_id=mate_id(dy, dz), device_id_type=MESH)
+    for copy in loaded[4:]:
+        copy.start()
     for copy in loaded[:4]:
         copy.wait()
     row_ids = lax.broadcasted_iota(jnp.int32, (8, 128), 0)
@@ -291,6 +292,13 @@
             device_id=mate_id(*twins[index]), device_id_type=MESH,
         )
 
+    def polar_arrival(index, c):
+        return pltpu.make_async_remote_copy(
+            src_ref=polar_hbm.at[0, c], dst_ref=polar_far.at[index, c],
+            send_sem=polar_send.at[index, c], recv_sem=polar_recv.at[index, c],
+            device_id=mate_id(0, turn), device_id_type=MESH,
+        )
+
     def onward_copy(c):
         return pltpu.make_async_remote_copy(
             src_ref=polar_far.at[my_core, c], dst_ref=polar_far.at[2, c],
@@ -304,8 +312,7 @@
                 polar_copy(index, c).start()
 
     def pass_on(c):
-        for index in range(2):
-            polar_copy(index, c).wait_recv()
+        polar_arrival(my_core, c).wait_recv()
         onward_copy(c).start()
 
     for step in range(1, groups):
@@ -529,34 +536,44 @@
             if after == plain * ny + place + 1 and after > plain * ny:
                 pass_on(c + 1)
 
-    for group in range(ngy * groups_here):
-        twin_copy(group).wait_recv()
-    for c in range(1, channels + 1):
-        if c < channels:
-            polar_copy(2, c).wait_recv()
-        else:
-            polar_copy(2, 0).wait_recv()
+    for c in range(channels):
+        polar_arrival(1 - my_core, c).wait_recv()
+        polar_arrival(2, c).wait_recv()
     twin_load = my_load + turn
     slopes = [slot_value(my_load, TANGENT), slot_value(twin_load, TANGENT)]
     totals_of = [[jnp.zeros((z_here, nx), f32) for _ in range(strains)] for _ in range(2)]
     counted = jnp.zeros((z_here, nx), f32)
-    for index, (dy, dz) in enumerate([(0, 0)] + twins):
-        part = lax.rem(my_z // CORES + dz // CORES, ngz // CORES)
-        for y in range(y_here):
-            row = dy * y_here + y
-            z_at = pl.ds(pl.multiple_of((CORES * part + my_core) * z_here, 8), z_here)
-            second = phase_all[row, z_at, :] == 1
-            counted = counted + jnp.where(second, 1.0, 0.0)
-            mods = [jnp.where(second, slope, 1.0) for slope in slopes]
-            for c in range(channels):
-                theirs = twin_field[c, row, part]
-                if index == 0:
-                    fields[0, twin_load, c, y] = theirs
-                fluxes = [mods[0] * field_now[c, row, part, my_core], mods[1] * theirs]
-                for j in range(strains):
-                    weight = polar[c, j, y] if index == 0 else polar_far[index - 1, c, j, y]
-                    for which in range(2):
-                        totals_of[which][j] = totals_of[which][j] + weight * fluxes[which]
+    corners = [(0, 0)] + twins
+    arrived = []
+    for _, row in order[-ny:]:
+        if row // SENT_ROWS not in arrived:
+            arrived.append(row // SENT_ROWS)
+    for which in range(2):
+        for group in arrived:
+            if which:
+                twin_copy(group).wait_recv()
+            for index, (dy, dz) in enumerate(corners):
+                if dy != group // groups_here:
+                    continue
+                part = lax.rem(my_z // CORES + dz // CORES, ngz // CORES)
+                for row in range(group * SENT_ROWS, (group + 1) * SENT_ROWS):
+                    y = row % y_here
+                    z_at = pl.ds(pl.multiple_of((CORES * part + my_core) * z_here, 8), z_here)
+                    second = phase_all[row, z_at, :] == 1
+                    mod = jnp.where(second, slopes[which], 1.0)
+                    if not which:
+                        counted = counted + jnp.where(second, 1.0, 0.0)
+                    for c in range(channels):
+                        if which:
+                            value = twin_field[c, row, part]
+                            if index == 0:
+                                fields[0, twin_load, c, y] = value
+                        else:
+                            value = field_now[c, row, part, my_core]
+                        flux = mod * value
+                        for j in range(strains):
+                            weight = polar[c, j, y] if index == 0 else polar_far[index - 1, c, j, y]
+                            totals_of[which][j] = totals_of[which][j] + weight * flux
 
     def whole_sum(values):
         return jnp.sum(jnp.sum(values, axis=0, keepdims=True), axis=1, keepdims=True)

time: 32.6 us -> 32.5 us (level)
  no operation moved by 1% of the time
where the time goes in v4:
time: 32.5 us; the launch traced here: 32.3 us
  Pallas kernels  31.7 us (98%)
  between operations  0.64 us (2%)
    pallas_call x1, Pallas kernels, fused_body(): pl.pallas_call(functools.partial(kernel, groups, ngy, ngz), out_shape=(ja...  30.9 us
    pallas_call x1, Pallas kernels, fused_body(): pl.pallas_call(deliver, out_shape=(jax.ShapeDtypeStruct(held_fields.shape...  0.77 us

profile of v4, /device:TPU:0, one launch (start us, length us, event | category | flops | bytes accessed | tf_op | source)
XLA Modules:
  0.0 32.3 jit_solution(14190660224072886230)
XLA Ops:
  0.6 30.9 %shard_map.86 = (f32[1,8,3,4,8,128]{5,4,3,2,1,0:T(8,128)S(1)}, f32[4,6]{1,0:T(4,128)S(1)}) custom-call(f32[8,6]{1,0:T(8,128)} %strain_hbm.1, f32[8]{0:T(128)} %tangent_hbm.1, s32[4]{0:T(128)} %yield_hbm.1, s32[4]{0:T(128)} %bitcast.1, f32[3,3,27]{2,1,0:T(4,128)} %stencil_hbm.1, s32[1,4,8,128]{3,2,1,0:T(8,128)} %phase_hbm.1, f32[1,3,6,4,8,128]{5,4,3,2,1,0:T(8,128)} %polar_hbm.1), custom_call_target="tpu_custom_call" | custom-call | tf_op jit(solution)/shard_map/pallas_call | solution.py:692
  31.6 0.8 %shard_map.87 = (f32[1,8,3,4,8,128]{5,4,3,2,1,0:T(8,128)}, f32[4,6]{1,0:T(4,128)}) custom-call(f32[1,8,3,4,8,128]{5,4,3,2,1,0:T(8,128)S(1)} %get-tuple-element.4.held_fields, f32[4,6]{1,0:T(4,128)S(1)} %get-tuple-element.5.held_rows), custom_call_target="tpu_custom_call" | custom-call | tf_op jit(solution)/shard_map/pallas_call | solution.py:738

commit v5 on v4

--- a/solution.py
+++ b/solution.py
@@ -10,7 +10,8 @@
 CAP = 2
 CORES = 2
 SKEWED = 1
-PASSES = (16, 24)
+PASSES = (16,)
+STRAIGHT = (2,)
 SENT_ROWS = 2
 SWEEPS = 6
 MESH = pl.DeviceIdType.MESH
@@ -308,7 +309,7 @@
 
     def send_polar(channels_now):
         for c in channels_now:
-            for index in range(2):
+            for index in range(3 if c in STRAIGHT else 2):
                 polar_copy(index, c).start()
 
     def pass_on(c):
@@ -538,6 +539,8 @@
 
     for c in range(channels):
         polar_arrival(1 - my_core, c).wait_recv()
+        if c in STRAIGHT:
+            polar_arrival(my_core, c).wait_recv()
         polar_arrival(2, c).wait_recv()
     twin_load = my_load + turn
     slopes = [slot_value(my_load, TANGENT), slot_value(twin_load, TANGENT)]
@@ -642,7 +645,7 @@
     for c in range(channels):
         for index in range(2):
             polar_copy(index, c).wait_send()
-        onward_copy(c).wait_send()
+        (polar_copy(2, c) if c in STRAIGHT else onward_copy(c)).wait_send()
     for group in range(groups_here):
         own_field(group).wait()
     for step in range(1, groups):

time: 32.5 us -> 32.3 us (level)
  no operation moved by 1% of the time
where the time goes in v5:
time: 32.3 us; the launch traced here: 32.2 us
  Pallas kernels  31.5 us (98%)
  between operations  0.64 us (2%)
    pallas_call x1, Pallas kernels, fused_body(): pl.pallas_call(functools.partial(kernel, groups, ngy, ngz), out_shape=(ja...  30.7 us
    pallas_call x1, Pallas kernels, fused_body(): pl.pallas_call(deliver, out_shape=(jax.ShapeDtypeStruct(held_fields.shape...  0.77 us

profile of v5, /device:TPU:0, one launch (start us, length us, event | category | flops | bytes accessed | tf_op | source)
XLA Modules:
  0.0 32.2 jit_solution(11658071573442281066)
XLA Ops:
  0.6 30.7 %shard_map.86 = (f32[1,8,3,4,8,128]{5,4,3,2,1,0:T(8,128)S(1)}, f32[4,6]{1,0:T(4,128)S(1)}) custom-call(f32[8,6]{1,0:T(8,128)} %strain_hbm.1, f32[8]{0:T(128)} %tangent_hbm.1, s32[4]{0:T(128)} %yield_hbm.1, s32[4]{0:T(128)} %bitcast.1, f32[3,3,27]{2,1,0:T(4,128)} %stencil_hbm.1, s32[1,4,8,128]{3,2,1,0:T(8,128)} %phase_hbm.1, f32[1,3,6,4,8,128]{5,4,3,2,1,0:T(8,128)} %polar_hbm.1), custom_call_target="tpu_custom_call" | custom-call | tf_op jit(solution)/shard_map/pallas_call | solution.py:695
  31.4 0.8 %shard_map.87 = (f32[1,8,3,4,8,128]{5,4,3,2,1,0:T(8,128)}, f32[4,6]{1,0:T(4,128)}) custom-call(f32[1,8,3,4,8,128]{5,4,3,2,1,0:T(8,128)S(1)} %get-tuple-element.4.held_fields, f32[4,6]{1,0:T(4,128)S(1)} %get-tuple-element.5.held_rows), custom_call_target="tpu_custom_call" | custom-call | tf_op jit(solution)/shard_map/pallas_call | solution.py:741
